TPU v7x, 256 devices: a whole 4x4x8 slice. The times are simulated.
256 devices in a mesh: span: 16 (over z_hi, y, core), seq: 16 (over z_lo, x).
Axes of the slice: x: 4, y: 4, z: 8 (z_hi: 2, z_lo: 4; z = z_hi * 4 + z_lo), core: 2. Of those that a mesh axis runs over, the one named last changes fastest.
Arguments:
- query_rows: bfloat16 [12288, 4096], P(('span', 'seq')), may hold values from -8 to 8
- key_rows: bfloat16 [12288, 4096], P(('span', 'seq')), may hold values from -8 to 8
- value_rows: bfloat16 [12288, 4096], P(('span', 'seq')), may hold values from -8 to 8
- token_counts: int32 [16], replicated, may hold values from 384 to 768, as said below
Outputs:
- attended: bfloat16 [12288, 4096], P(('span', 'seq'))
Inputs may be any that keep to these rules, and one draw needn't show every extreme that they name: token_counts[b] is the number of real tokens of span b; some span is full.
All inputs are finite; a program needn't handle non-finite values.
Results may differ from a plain program's by a relative error of at most 0.0075.
Values may be sent and summed in bfloat16 or wider, within the bound.
A program may use at most 64 MiB of HBM per device.

v0:
```python
import jax
import jax.numpy as jnp
from jax import lax
from jax.sharding import PartitionSpec as P

HD = 128


def on_device(query_rows, key_rows, value_rows, token_counts):
    tok_rows = query_rows.shape[0]
    row_width = query_rows.shape[1]
    heads_all = row_width // HD
    scaling = HD ** (-0.5)
    query_split = query_rows.reshape(tok_rows, heads_all, HD)
    key_split = key_rows.reshape(tok_rows, heads_all, HD)
    value_split = value_rows.reshape(tok_rows, heads_all, HD)
    query_heads, key_heads, value_heads = (
        lax.all_to_all(query_split, "seq", split_axis=1, concat_axis=0, tiled=True),
        lax.all_to_all(key_split, "seq", split_axis=1, concat_axis=0, tiled=True),
        lax.all_to_all(value_split, "seq", split_axis=1, concat_axis=0, tiled=True),
    )
    span_len = query_heads.shape[0]
    heads_dev = query_heads.shape[1]
    own_span = lax.axis_index("span")

    def valid_count(span_id):
        listed = jnp.arange(token_counts.shape[0], dtype=jnp.int32)
        return jnp.sum(jnp.where(listed == span_id, token_counts, 0))

    def attend(carried, key_block, value_block, span_id):
        running_max, denominator, numerator = carried
        scores = (
            jnp.einsum("qhd,khd->qhk", query_heads, key_block, preferred_element_type=jnp.float32)
            * scaling
        )
        key_valid = jnp.arange(span_len, dtype=jnp.int32) < valid_count(span_id)
        scores = jnp.where(key_valid[None, None, :], scores, -1e30)
        new_max = jnp.maximum(running_max, jnp.max(scores, axis=2))
        shrink = jnp.exp(running_max - new_max)
        weights = jnp.where(
            key_valid[None, None, :], jnp.exp(scores - new_max[:, :, None]), 0.0
        ).astype(jnp.bfloat16)
        denominator = denominator * shrink + jnp.sum(weights.astype(jnp.float32), axis=2)
        numerator = numerator * shrink[:, :, None] + jnp.einsum(
            "qhk,khd->qhd", weights, value_block, preferred_element_type=jnp.float32
        )
        return (new_max, denominator, numerator)

    def attend_if(carried, key_block, value_block, span_id):
        wanted = jnp.logical_and(span_id <= own_span, span_id >= 0)
        return lax.cond(
            wanted,
            lambda state_in: attend(state_in, key_block, value_block, span_id),
            lambda state_in: state_in,
            carried,
        )

    initial = (
        jnp.full((span_len, heads_dev), -1e30, jnp.float32),
        jnp.zeros((span_len, heads_dev), jnp.float32),
        jnp.zeros((span_len, heads_dev, HD), jnp.float32),
    )
    carried = initial
    key_piece = lax.all_gather(key_heads, "span", axis=0, tiled=True)
    value_piece = lax.all_gather(value_heads, "span", axis=0, tiled=True)
    block_count = key_piece.shape[0] // span_len
    key_stack = key_piece.reshape(block_count, span_len, heads_dev, HD)
    value_stack = value_piece.reshape(block_count, span_len, heads_dev, HD)

    def one_block(state_in, block_item):
        position, key_item, value_item = block_item
        return (attend_if(state_in, key_item, value_item, position), None)

    carried, unused = lax.scan(
        one_block, carried, (jnp.arange(block_count, dtype=jnp.int32), key_stack, value_stack)
    )
    running_max, denominator, numerator = carried
    averaged = (numerator / denominator[:, :, None]).astype(jnp.bfloat16)
    returned = lax.all_to_all(averaged, "seq", split_axis=0, concat_axis=1, tiled=True)
    return returned.reshape(tok_rows, row_width)


def solution(mesh):
    return jax.shard_map(
        on_device,
        mesh=mesh,
        in_specs=(
            P(("span", "seq"), None),
            P(("span", "seq"), None),
            P(("span", "seq"), None),
            P(),
        ),
        out_specs=P(("span", "seq"), None),
        check_vma=False,
    )
```

profile of v0, /device:TPU:153, one launch (start us, length us, event | category | flops | bytes accessed | tf_op | source)
XLA Modules:
  0.0 389.6 jit_solution(16366207792122076116)
XLA Ops:
  7.6 17.0 %all_to_all.69 = bf16[48,32,128]{2,0,1:T(8,128)(2,1)S(1)} all-to-all(bf16[48,32,128]{2,0,1:T(8,128)(2,1)S(1)} %copy_bitcast_fusion.2), channel_id=1, replica_groups=mesh['span'=16,'seq'=16] {'seq'}, dimensions={1} | all-to-all | bytes 786432 | tf_op jit(solution)/shard_map/all_to_all | solution.py:19
  26.5 15.5 %all_to_all.70 = bf16[48,32,128]{2,0,1:T(8,128)(2,1)S(1)} all-to-all(bf16[48,32,128]{2,0,1:T(8,128)(2,1)S(1)} %copy_bitcast_fusion), channel_id=1, replica_groups=mesh['span'=16,'seq'=16] {'seq'}, dimensions={1} | all-to-all | bytes 786432 | tf_op jit(solution)/shard_map/all_to_all | solution.py:20
  48.8 10.0 %all-to-all-done.1 = bf16[48,32,128]{2,0,1:T(8,128)(2,1)S(1)} async-done(((bf16[48,32,128]{2,0,1:T(8,128)(2,1)}), bf16[48,32,128]{2,0,1:T(8,128)(2,1)S(1)}, u32[]{:S(2)}, u32[]{:S(2)}) %all-to-all-start.1) | async-done | bytes 393248 | tf_op jit(solution)/shard_map/all_to_all | solution.py:18
  58.8 48.6 %all-gather.3.cloned.1.call-done = bf16[12288,2,128]{2,0,1:T(8,128)(2,1)} async-done(((bf16[768,2,128]{2,0,1:T(8,128)(2,1)}), bf16[12288,2,128]{2,0,1:T(8,128)(2,1)}) %all-gather.3.cloned.1.call-update) | async-done | bytes 6291472 | tf_op jit(solution)/shard_map/all_gather | solution.py:64
  107.4 6.1 %copy.48 = bf16[16,768,2,128]{3,1,2,0:T(8,128)(2,1)} copy(bf16[16,768,2,128]{3,1,0,2:T(8,128)(2,1)} %bitcast.60) | data formatting | bytes 12582912 | tf_op jit(solution)/shard_map/while | solution.py:74
  113.5 84.8 %all-gather.5.cloned.1.call-done = bf16[12288,2,128]{2,0,1:T(8,128)(2,1)} async-done(((bf16[768,2,128]{2,0,1:T(8,128)(2,1)}), bf16[12288,2,128]{2,0,1:T(8,128)(2,1)}) %all-gather.5.cloned.1.call-update) | async-done | bytes 6291472 | tf_op jit(solution)/shard_map/all_gather | solution.py:65
  204.6 153.3 %while.14 = (s32[]{:T(128)}, f32[768,2]{0,1:T(2,128)S(1)}, f32[768,2]{0,1:T(2,128)S(1)}, f32[768,2,128]{2,0,1:T(8,128)S(1)}, s32[16]{0:T(128)S(1)}, /*index=5*/s...) while((s32[]{:T(128)}, f32[768,2]{0,1:T(2,128)S(1)}, ...), condition=%wide.region_6.7_spmd, body=%wide.region_0.6_spmd.sunk | while | flops 616173312 | bytes 17004136 | solution.py:74
  206.5 7.7 %conditional.2 = ((f32[768,2]{0,1:T(2,128)S(1)}, f32[768,2]{0,1:T(2,128)S(1)}, f32[768,2,128]{2,0,1:T(8,128)S(1)})) conditional(s32[]{:T(128)} %convert_element_type.22, (f32[768,2]{0,1:T(2,128)S(1)}, f32[768,2]{0,1:T(2,128)S(1)}, f32[768,2,128]{2,0,1:T(8,128)S(1)}) %tuple.39, (s32[]{:T(128)}, s32[16]{0:T(128)S(1)}, ...), branch_computations={%region_1.1_spmd, %region_2.5_spmd} | conditional | flops 616173312 | bytes 17003884 | solution.py:51
  216.0 7.7 %conditional.2 = ((f32[768,2]{0,1:T(2,128)S(1)}, f32[768,2]{0,1:T(2,128)S(1)}, f32[768,2,128]{2,0,1:T(8,128)S(1)})) conditional(s32[]{:T(128)} %convert_element_type.22, (f32[768,2]{0,1:T(2,128)S(1)}, f32[768,2]{0,1:T(2,128)S(1)}, f32[768,2,128]{2,0,1:T(8,128)S(1)}) %tuple.39, (s32[]{:T(128)}, s32[16]{0:T(128)S(1)}, ...), branch_computations={%region_1.1_spmd, %region_2.5_spmd} | conditional | flops 616173312 | bytes 17003884 | solution.py:51
  225.6 7.7 %conditional.2 = ((f32[768,2]{0,1:T(2,128)S(1)}, f32[768,2]{0,1:T(2,128)S(1)}, f32[768,2,128]{2,0,1:T(8,128)S(1)})) conditional(s32[]{:T(128)} %convert_element_type.22, (f32[768,2]{0,1:T(2,128)S(1)}, f32[768,2]{0,1:T(2,128)S(1)}, f32[768,2,128]{2,0,1:T(8,128)S(1)}) %tuple.39, (s32[]{:T(128)}, s32[16]{0:T(128)S(1)}, ...), branch_computations={%region_1.1_spmd, %region_2.5_spmd} | conditional | flops 616173312 | bytes 17003884 | solution.py:51
  235.2 7.7 %conditional.2 = ((f32[768,2]{0,1:T(2,128)S(1)}, f32[768,2]{0,1:T(2,128)S(1)}, f32[768,2,128]{2,0,1:T(8,128)S(1)})) conditional(s32[]{:T(128)} %convert_element_type.22, (f32[768,2]{0,1:T(2,128)S(1)}, f32[768,2]{0,1:T(2,128)S(1)}, f32[768,2,128]{2,0,1:T(8,128)S(1)}) %tuple.39, (s32[]{:T(128)}, s32[16]{0:T(128)S(1)}, ...), branch_computations={%region_1.1_spmd, %region_2.5_spmd} | conditional | flops 616173312 | bytes 17003884 | solution.py:51
  244.8 7.7 %conditional.2 = ((f32[768,2]{0,1:T(2,128)S(1)}, f32[768,2]{0,1:T(2,128)S(1)}, f32[768,2,128]{2,0,1:T(8,128)S(1)})) conditional(s32[]{:T(128)} %convert_element_type.22, (f32[768,2]{0,1:T(2,128)S(1)}, f32[768,2]{0,1:T(2,128)S(1)}, f32[768,2,128]{2,0,1:T(8,128)S(1)}) %tuple.39, (s32[]{:T(128)}, s32[16]{0:T(128)S(1)}, ...), branch_computations={%region_1.1_spmd, %region_2.5_spmd} | conditional | flops 616173312 | bytes 17003884 | solution.py:51
  254.4 7.7 %conditional.2 = ((f32[768,2]{0,1:T(2,128)S(1)}, f32[768,2]{0,1:T(2,128)S(1)}, f32[768,2,128]{2,0,1:T(8,128)S(1)})) conditional(s32[]{:T(128)} %convert_element_type.22, (f32[768,2]{0,1:T(2,128)S(1)}, f32[768,2]{0,1:T(2,128)S(1)}, f32[768,2,128]{2,0,1:T(8,128)S(1)}) %tuple.39, (s32[]{:T(128)}, s32[16]{0:T(128)S(1)}, ...), branch_computations={%region_1.1_spmd, %region_2.5_spmd} | conditional | flops 616173312 | bytes 17003884 | solution.py:51
  263.9 7.7 %conditional.2 = ((f32[768,2]{0,1:T(2,128)S(1)}, f32[768,2]{0,1:T(2,128)S(1)}, f32[768,2,128]{2,0,1:T(8,128)S(1)})) conditional(s32[]{:T(128)} %convert_element_type.22, (f32[768,2]{0,1:T(2,128)S(1)}, f32[768,2]{0,1:T(2,128)S(1)}, f32[768,2,128]{2,0,1:T(8,128)S(1)}) %tuple.39, (s32[]{:T(128)}, s32[16]{0:T(128)S(1)}, ...), branch_computations={%region_1.1_spmd, %region_2.5_spmd} | conditional | flops 616173312 | bytes 17003884 | solution.py:51
  273.5 7.7 %conditional.2 = ((f32[768,2]{0,1:T(2,128)S(1)}, f32[768,2]{0,1:T(2,128)S(1)}, f32[768,2,128]{2,0,1:T(8,128)S(1)})) conditional(s32[]{:T(128)} %convert_element_type.22, (f32[768,2]{0,1:T(2,128)S(1)}, f32[768,2]{0,1:T(2,128)S(1)}, f32[768,2,128]{2,0,1:T(8,128)S(1)}) %tuple.39, (s32[]{:T(128)}, s32[16]{0:T(128)S(1)}, ...), branch_computations={%region_1.1_spmd, %region_2.5_spmd} | conditional | flops 616173312 | bytes 17003884 | solution.py:51
  283.1 7.7 %conditional.2 = ((f32[768,2]{0,1:T(2,128)S(1)}, f32[768,2]{0,1:T(2,128)S(1)}, f32[768,2,128]{2,0,1:T(8,128)S(1)})) conditional(s32[]{:T(128)} %convert_element_type.22, (f32[768,2]{0,1:T(2,128)S(1)}, f32[768,2]{0,1:T(2,128)S(1)}, f32[768,2,128]{2,0,1:T(8,128)S(1)}) %tuple.39, (s32[]{:T(128)}, s32[16]{0:T(128)S(1)}, ...), branch_computations={%region_1.1_spmd, %region_2.5_spmd} | conditional | flops 616173312 | bytes 17003884 | solution.py:51
  292.7 7.7 %conditional.2 = ((f32[768,2]{0,1:T(2,128)S(1)}, f32[768,2]{0,1:T(2,128)S(1)}, f32[768,2,128]{2,0,1:T(8,128)S(1)})) conditional(s32[]{:T(128)} %convert_element_type.22, (f32[768,2]{0,1:T(2,128)S(1)}, f32[768,2]{0,1:T(2,128)S(1)}, f32[768,2,128]{2,0,1:T(8,128)S(1)}) %tuple.39, (s32[]{:T(128)}, s32[16]{0:T(128)S(1)}, ...), branch_computations={%region_1.1_spmd, %region_2.5_spmd} | conditional | flops 616173312 | bytes 17003884 | solution.py:51
  302.3 7.7 %conditional.2 = ((f32[768,2]{0,1:T(2,128)S(1)}, f32[768,2]{0,1:T(2,128)S(1)}, f32[768,2,128]{2,0,1:T(8,128)S(1)})) conditional(s32[]{:T(128)} %convert_element_type.22, (f32[768,2]{0,1:T(2,128)S(1)}, f32[768,2]{0,1:T(2,128)S(1)}, f32[768,2,128]{2,0,1:T(8,128)S(1)}) %tuple.39, (s32[]{:T(128)}, s32[16]{0:T(128)S(1)}, ...), branch_computations={%region_1.1_spmd, %region_2.5_spmd} | conditional | flops 616173312 | bytes 17003884 | solution.py:51
  311.8 7.7 %conditional.2 = ((f32[768,2]{0,1:T(2,128)S(1)}, f32[768,2]{0,1:T(2,128)S(1)}, f32[768,2,128]{2,0,1:T(8,128)S(1)})) conditional(s32[]{:T(128)} %convert_element_type.22, (f32[768,2]{0,1:T(2,128)S(1)}, f32[768,2]{0,1:T(2,128)S(1)}, f32[768,2,128]{2,0,1:T(8,128)S(1)}) %tuple.39, (s32[]{:T(128)}, s32[16]{0:T(128)S(1)}, ...), branch_computations={%region_1.1_spmd, %region_2.5_spmd} | conditional | flops 616173312 | bytes 17003884 | solution.py:51
  321.4 7.7 %conditional.2 = ((f32[768,2]{0,1:T(2,128)S(1)}, f32[768,2]{0,1:T(2,128)S(1)}, f32[768,2,128]{2,0,1:T(8,128)S(1)})) conditional(s32[]{:T(128)} %convert_element_type.22, (f32[768,2]{0,1:T(2,128)S(1)}, f32[768,2]{0,1:T(2,128)S(1)}, f32[768,2,128]{2,0,1:T(8,128)S(1)}) %tuple.39, (s32[]{:T(128)}, s32[16]{0:T(128)S(1)}, ...), branch_computations={%region_1.1_spmd, %region_2.5_spmd} | conditional | flops 616173312 | bytes 17003884 | solution.py:51
  331.0 7.7 %conditional.2 = ((f32[768,2]{0,1:T(2,128)S(1)}, f32[768,2]{0,1:T(2,128)S(1)}, f32[768,2,128]{2,0,1:T(8,128)S(1)})) conditional(s32[]{:T(128)} %convert_element_type.22, (f32[768,2]{0,1:T(2,128)S(1)}, f32[768,2]{0,1:T(2,128)S(1)}, f32[768,2,128]{2,0,1:T(8,128)S(1)}) %tuple.39, (s32[]{:T(128)}, s32[16]{0:T(128)S(1)}, ...), branch_computations={%region_1.1_spmd, %region_2.5_spmd} | conditional | flops 616173312 | bytes 17003884 | solution.py:51
  340.6 7.7 %conditional.2 = ((f32[768,2]{0,1:T(2,128)S(1)}, f32[768,2]{0,1:T(2,128)S(1)}, f32[768,2,128]{2,0,1:T(8,128)S(1)})) conditional(s32[]{:T(128)} %convert_element_type.22, (f32[768,2]{0,1:T(2,128)S(1)}, f32[768,2]{0,1:T(2,128)S(1)}, f32[768,2,128]{2,0,1:T(8,128)S(1)}) %tuple.39, (s32[]{:T(128)}, s32[16]{0:T(128)S(1)}, ...), branch_computations={%region_1.1_spmd, %region_2.5_spmd} | conditional | flops 616173312 | bytes 17003884 | solution.py:51
  350.2 7.7 %conditional.2 = ((f32[768,2]{0,1:T(2,128)S(1)}, f32[768,2]{0,1:T(2,128)S(1)}, f32[768,2,128]{2,0,1:T(8,128)S(1)})) conditional(s32[]{:T(128)} %convert_element_type.22, (f32[768,2]{0,1:T(2,128)S(1)}, f32[768,2]{0,1:T(2,128)S(1)}, f32[768,2,128]{2,0,1:T(8,128)S(1)}) %tuple.39, (s32[]{:T(128)}, s32[16]{0:T(128)S(1)}, ...), branch_computations={%region_1.1_spmd, %region_2.5_spmd} | conditional | flops 616173312 | bytes 17003884 | solution.py:51
  358.5 22.9 %all_to_all.71 = bf16[768,2,128]{2,1,0:T(2,128)(2,1)S(1)} all-to-all(bf16[768,2,128]{2,1,0:T(2,128)(2,1)S(1)} %copy.50), channel_id=1, replica_groups=mesh['span'=16,'seq'=16] {'seq'}, dimensions={0} | all-to-all | bytes 786432 | tf_op jit(solution)/shard_map/all_to_all | solution.py:79
  (170 shorter events, 149.1 us)
Async XLA Ops:
  6.5 1.0 copy-start
  6.5 36.2 %copy-start.1 = (bf16[48,4096]{1,0:T(8,128)(2,1)S(1)}, bf16[48,4096]{1,0:T(8,128)(2,1)}, u32[]{:S(2)}) copy-start(bf16[48,4096]{1,0:T(8,128)(2,1)} %param.8) | copy-start | bytes 1179652
  6.5 100.9 %all-gather.3.cloned.1.call-start = ((), (), s32[]{:S(2)}) async-start(), calls=%async_computation.4 | async-start | bytes 6684672 | tf_op jit(solution)/shard_map/all_gather | solution.py:64
  25.4 173.0 %all-gather.5.cloned.1.call-start = ((), (), s32[]{:S(2)}) async-start(), calls=%async_computation.5 | async-start | bytes 6684672 | tf_op jit(solution)/shard_map/all_gather | solution.py:65
  43.6 15.2 %all-to-all-start.1 = ((bf16[48,32,128]{2,0,1:T(8,128)(2,1)}), bf16[48,32,128]{2,0,1:T(8,128)(2,1)S(1)}, u32[]{:S(2)}, u32[]{:S(2)}) async-start(bf16[48,32,128]{2,0,1:T(8,128)(2,1)} %copy_bitcast_fusion.1), calls=%async_computation.1 | async-start | bytes 786432 | tf_op jit(solution)/shard_map/all_to_all | solution.py:18
  198.3 6.2 %copy-start.2 = (s32[16]{0:T(128)S(1)}, s32[16]{0:T(128)}, u32[]{:S(2)}) copy-start(s32[16]{0:T(128)} %param.11) | copy-start | bytes 196
Sparse Core Ops, SparseCore 0:
  25.5 81.8 all-gather.2
  110.2 88.1 all-gather.4
where the time goes:
time: 392 us; the launch traced here: 390 us
  waiting for transfers between devices  143 us (36%)
  matrix products  65.9 us (17%)
  other arithmetic  56.1 us (14%)
  blocking collectives  55.3 us (14%)
  local copies, waits for them, and re-layouts  28 us (7%)
  loops' own time  22.2 us (6%)
  between operations  13.5 us (3%)
  starting transfers between devices  5.26 us (1%)
    all_gather x1, waiting for transfers between devices, on_device(): value_piece = lax.all_gather(value_heads, 'span', axis=0, tiled=True)  84.8 us
    all_gather x1, waiting for transfers between devices, on_device(): key_piece = lax.all_gather(key_heads, 'span', axis=0, tiled=True)  48.6 us
    dot_general x16, matrix products, attend(): jnp.einsum('qhk,khd->qhd', weights, value_block, preferred_element_type=j...  36.8 us
    dot_general x16, matrix products, attend(): jnp.einsum('qhd,khd->qhk', query_heads, key_block, preferred_element_type...  29.1 us
    reduce_sum x16, other arithmetic, attend(): jnp.sum(weights.astype(jnp.float32), axis=2)  26.5 us
    all_to_all x1, blocking collectives, on_device(): lax.all_to_all(averaged, 'seq', split_axis=0, concat_axis=1, tiled=True)  22.9 us
    another operation x1, loops' own time, on_device(): lax.scan(one_block, carried, (jnp.arange(block_count, dtype=jnp.int32), k...  21.2 us
    reduce_sum x16, other arithmetic, valid_count(): return jnp.sum(jnp.where(listed == span_id, token_counts, 0))  20 us
  transfers between devices with their start and end apart: 3, of which 3 were waited for; matrix products, arithmetic and copies ran while one was open for 2% of the time, Pallas kernels for 0%

commit v1 on v0

v1 whole, which is shorter than its diff:
```python
import functools
import math

import jax
import jax.numpy as jnp
from jax import lax
from jax.experimental import pallas as pl
from jax.experimental.pallas import tpu as pltpu
from jax.sharding import PartitionSpec as P

MESH = pl.DeviceIdType.MESH
HD = 128
SPANS = 16
LEN = 768
ROWS = 48
PART = 192
PEERS = 32
NEG = -1e30
LOG2_SCALE = HD ** -0.5 * math.log2(math.e)
VMEM_LIMIT = 56 * 1024 * 1024


class Place:
    def __init__(self):
        self.span = lax.axis_index("span")
        self.seq = lax.axis_index("seq")
        self.core = self.span % 2
        self.y = (self.span // 2) % 4
        self.z = (self.span // 8) * 4 + self.seq // 4
        self.x = self.seq % 4

    def span_of(self, z_hi, y, core):
        return (z_hi * 4 + y) * 2 + core

    def plane(self, t):
        return (self.z + ((t + 1) // 2) * (2 * (t % 2) - 1) + 8) % 8

    def peers(self):
        places = {}
        xs = [self.x] + [(self.x + dx) % 4 for dx in (1, 2, 3)]
        for t in range(8):
            dz = ((t + 1) // 2) * (2 * (t % 2) - 1)
            z = (self.z + dz + 8) % 8
            z_hi, z_lo = z // 4, z % 4
            span = self.span_of(z_hi, self.y, self.core)
            for dx in range(4):
                seq = z_lo * 4 + xs[dx]
                places[t, dx] = ((span, seq), z_hi * 16 + seq)
        return places

    def group(self, g):
        z_hi, z_lo = self.z // 4, self.z % 4
        inner = ((z_lo + 1) // 2) % 2
        other = jnp.where(g == 0, 0, jnp.where(g == 1, 1 - inner, jnp.where(g == 2, inner, 1)))
        moved = jnp.where((g == 1) | (g == 2), 1, 0)
        return (z_hi + other) % 2, (z_lo // 2 + moved) % 2

    def up(self):
        return (self.span_of(self.z // 4, (self.y + 1) % 4, self.core), self.seq)

    def down(self):
        return (self.span_of(self.z // 4, (self.y + 3) % 4, self.core), self.seq)

    def sibling(self):
        return (self.span_of(self.z // 4, self.y, 1 - self.core), self.seq)


def greet(devices):
    barrier = pltpu.get_barrier_semaphore()
    for device in devices:
        pl.semaphore_signal(barrier, inc=1, device_id=device, device_id_type=MESH)
    pl.semaphore_wait(barrier, len(devices))


def remote(src, dst, send_sem, recv_sem, device):
    return pltpu.make_async_remote_copy(
        src_ref=src, dst_ref=dst, send_sem=send_sem, recv_sem=recv_sem,
        device_id=device, device_id_type=MESH)


def arrived(ref, sem):
    pltpu.make_async_copy(ref, ref, sem).wait()


TILE = 256
HALF = LEN // 2


def attend_item(q_index, pair, half, keep_second, counts_ref, q2_ref, kv_ref, m_ref, acc_ref):
    rows = pl.ds(pl.multiple_of(half * HALF, 16), HALF)
    first, second = 2 * pair, 2 * pair + 1
    k = jnp.concatenate([kv_ref[0, first, rows], kv_ref[0, second, rows]], axis=0)
    k2 = jnp.concatenate([k, k], axis=1)
    v = jnp.concatenate([kv_ref[1, first, rows], kv_ref[1, second, rows]], axis=0)
    v2 = jnp.concatenate([v, jnp.ones_like(v)], axis=1)
    lane = lax.broadcasted_iota(jnp.int32, (1, HALF), 1) + half * HALF
    bias = jnp.concatenate([
        jnp.where(lane < counts_ref[first], 0.0, NEG),
        jnp.where(lane < counts_ref[second] * keep_second, 0.0, NEG)], axis=1)
    tiles = LEN // TILE
    scores, probs = [None] * tiles, [None] * tiles

    def at(i):
        return pl.ds(i * TILE, TILE)

    def score(i):
        scores[i] = lax.dot_general(
            q2_ref[q_index, at(i)], k2, (((1,), (1,)), ((), ())), preferred_element_type=jnp.float32)

    def soften(i):
        s = scores[i] + bias
        m_old = m_ref[q_index, at(i)]
        m_new = jnp.maximum(m_old, jnp.max(s, axis=1, keepdims=True))
        wide = jnp.concatenate([m_new] * (LEN // HD), axis=1)
        probs[i] = jnp.exp2(s - wide).astype(jnp.bfloat16)
        m_ref[q_index, at(i)] = m_new
        shrink = jnp.exp2(m_old - m_new)
        acc_ref[q_index, at(i)] = acc_ref[q_index, at(i)] * jnp.concatenate([shrink, shrink], axis=1)

    def gain(i):
        acc_ref[q_index, at(i)] += jnp.dot(probs[i], v2, preferred_element_type=jnp.float32)

    for i in range(tiles + 2):
        if i < tiles:
            score(i)
        if 1 <= i < tiles + 1:
            soften(i - 1)
        if 2 <= i:
            gain(i - 2)


def prepare(z_hi, q_ref, q2_ref, m_ref, acc_ref):
    q = q_ref[z_hi].astype(jnp.float32) * LOG2_SCALE
    high = q.astype(jnp.bfloat16)
    low = (q - high.astype(jnp.float32)).astype(jnp.bfloat16)
    q2_ref[z_hi] = jnp.concatenate([high, low], axis=1)
    m_ref[z_hi] = jnp.full((LEN, HD), NEG, jnp.float32)
    acc_ref[z_hi] = jnp.zeros((LEN, 2 * HD), jnp.float32)


MIRROR = (0, 2, 1, 4, 3, 6, 5, 7)


def messages(*planes):
    return [(t, dx) for dx in range(4) for t in planes if (t, dx) != (0, 0)]


def kernel(counts_ref, q_ref, k_ref, v_ref, out_ref, stage_q, stage_kv, qall, kvall, q2_ref, m_ref, acc_ref, o_ref,
           stage_sem, a2a_send, a2a_recv, q_recv, y_send, up_recv, down_recv, far_recv, sib_recv, o_send, o_recv):
    me = Place()
    up, down, sibling = me.up(), me.down(), me.sibling()
    peers = me.peers()
    own_head = peers[0, 0][1]
    staged = [
        pltpu.make_async_copy(k_ref, stage_kv.at[0], stage_sem.at[0]),
        pltpu.make_async_copy(v_ref, stage_kv.at[1], stage_sem.at[1]),
        pltpu.make_async_copy(q_ref, stage_q, stage_sem.at[2]),
    ]
    for copy in staged:
        copy.start()
    order = messages(0) + messages(1, 2) + messages(3, 4) + messages(5, 6) + messages(7)
    greet([peers[at][0] for at in order] + [up, down, sibling])

    def cols(head):
        return pl.ds(pl.multiple_of(head * HD, HD), HD)

    rows = pl.ds(pl.multiple_of(me.seq * ROWS, 16), ROWS)
    kv_rows = kvall.at[:, me.span, rows]
    q_rows = qall.at[me.z // 4, rows]

    def send_kv(places):
        for t, dx in places:
            device, head = peers[t, dx]
            remote(stage_kv.at[:, :, cols(head)], kv_rows, a2a_send.at[0], a2a_recv.at[MIRROR[t]], device).start()

    def send_q(places):
        for t, dx in places:
            device, head = peers[t, dx]
            remote(stage_q.at[:, cols(head)], q_rows, a2a_send.at[1], q_recv, device).start()

    y_up, y_down, y_far = (me.y + 1) % 4, (me.y + 3) % 4, (me.y + 2) % 4

    def block(t, y, core):
        z = me.plane(t)
        part = pl.ds(pl.multiple_of((z % 4) * PART, 16), PART)
        return me.span_of(z // 4, y, core), part

    def own_part(t):
        span, part = block(t, me.y, me.core)
        ref = kvall.at[:, span, part]
        arrived(ref, a2a_recv.at[t])
        remote(ref, ref, y_send.at[0], up_recv.at[t], up).start()
        remote(ref, ref, y_send.at[1], down_recv.at[t], down).start()
        remote(ref, ref, y_send.at[4], sib_recv.at[t], sibling).start()

    def near_part(t):
        span, part = block(t, y_down, me.core)
        ref = kvall.at[:, span, part]
        arrived(ref, up_recv.at[t])
        half = kvall.at[0, span, part]
        remote(half, half, y_send.at[2], far_recv.at[t], up).start()
        remote(ref, ref, y_send.at[4], sib_recv.at[8 + t], sibling).start()
        span, part = block(t, y_up, me.core)
        ref = kvall.at[:, span, part]
        arrived(ref, down_recv.at[t])
        half = kvall.at[1, span, part]
        remote(half, half, y_send.at[3], far_recv.at[t], down).start()
        remote(ref, ref, y_send.at[4], sib_recv.at[16 + t], sibling).start()

    def far_part(t):
        span, part = block(t, y_far, me.core)
        ref = kvall.at[:, span, part]
        arrived(ref, far_recv.at[t])
        remote(ref, ref, y_send.at[4], sib_recv.at[24 + t], sibling).start()

    def from_sibling(j, y, t):
        span, part = block(t, y, 1 - me.core)
        arrived(kvall.at[:, span, part], sib_recv.at[8 * j + t])

    def each(first, last, part):
        lax.fori_loop(first, last, lambda t, _: (part(t), 0)[1], 0)

    to = cols(own_head)

    def finish(h):
        o_ref[h] = (acc_ref[h, :, :HD] / acc_ref[h, :, HD:]).astype(jnp.bfloat16)

        @pl.when(me.z // 4 == h)
        def _():
            piece = o_ref.at[h, rows]
            pltpu.make_async_copy(piece, out_ref.at[:, to], o_recv).start()

        for place in order:
            device, head = peers[place]

            @pl.when(head // 16 == h)
            def _():
                piece = o_ref.at[h, pl.ds(pl.multiple_of((head % 16) * ROWS, 16), ROWS)]
                remote(piece, out_ref.at[:, to], o_send, o_recv, device).start()

    for copy in staged[:2]:
        copy.wait()
    pltpu.make_async_copy(stage_kv.at[:, :, to], kv_rows, a2a_recv.at[0]).start()
    send_kv(messages(0))
    send_kv(messages(1, 2))
    staged[2].wait()
    pltpu.make_async_copy(stage_q.at[:, to], q_rows, q_recv).start()
    send_q(order[:15])
    own_part(0)
    send_q(order[15:])
    own_part(1)
    own_part(2)
    send_kv(messages(3, 4))
    near_part(0)
    send_kv(messages(5, 6))
    send_kv(messages(7))
    near_part(1)
    near_part(2)
    each(0, 3, far_part)
    arrived(qall, q_recv)
    each(0, 2, lambda h: prepare(h, qall, q2_ref, m_ref, acc_ref))
    each(0, 1, functools.partial(from_sibling, 0, me.y))
    each(0, 1, functools.partial(from_sibling, 1, y_down))
    each(0, 1, functools.partial(from_sibling, 2, y_up))
    each(0, 1, functools.partial(from_sibling, 3, y_far))

    def step(i, _):
        g, j = i // 4, i % 4
        near, far = 2 * g + 1, jnp.minimum(2 * g + 3, 8)
        more, most = 2 * g + 3, jnp.where(g < 3, jnp.minimum(2 * g + 5, 8), 2 * g + 3)

        @pl.when(j == 0)
        def _():
            each(near, far, functools.partial(from_sibling, 0, me.y))

        @pl.when(j == 1)
        def _():
            each(more, jnp.minimum(more + 1, most), own_part)
            each(near, far, functools.partial(from_sibling, 1, y_down))

        @pl.when(j == 2)
        def _():
            each(more + 1, most, own_part)

            @pl.when(g >= 1)
            def _():
                each(near, far, far_part)

            each(near, far, functools.partial(from_sibling, 2, y_up))

        @pl.when(j == 3)
        def _():
            each(more, most, near_part)
            each(near, far, functools.partial(from_sibling, 3, y_far))

        y = (me.y + jnp.where(j == 0, 0, jnp.where(j == 1, 3, jnp.where(j == 2, 1, 2)))) % 4
        z_hi, half = me.group(g)
        pair = z_hi * 4 + y

        def item(q_index, _):
            own = q_index * 4 + me.y

            @pl.when(pair <= own)
            def _():
                keep = jnp.where((pair < own) | (me.core == 1), 1, 0)
                attend_item(q_index, pair, half, keep, counts_ref, q2_ref, kvall, m_ref, acc_ref)

            return 0

        lax.fori_loop(0, 2, item, 0)

        @pl.when((i == 11) & (me.z < 4))
        def _():
            finish(0)

        return 0

    lax.fori_loop(0, 16, step, 0)

    @pl.when(me.z >= 4)
    def _():
        finish(0)

    finish(1)

    sent = pl.ds(0, (PEERS - 1) * HD)
    arrived(stage_kv.at[:, :, sent], a2a_send.at[0])
    arrived(stage_q.at[:, sent], a2a_send.at[1])
    for j, ref in enumerate((kvall.at[:, 0:2], kvall.at[:, 0:2], kvall.at[0, 0:2], kvall.at[0, 0:2], kvall.at[:, 0:8])):
        arrived(ref, y_send.at[j])
    arrived(out_ref, o_recv)
    arrived(out_ref.at[:, sent], o_send)


def on_device(query_rows, key_rows, value_rows, token_counts):
    any_spec = pl.BlockSpec(memory_space=pl.ANY)
    dma = pltpu.SemaphoreType.DMA
    return pl.pallas_call(
        kernel,
        out_shape=jax.ShapeDtypeStruct((ROWS, PEERS * HD), jnp.bfloat16),
        in_specs=[pl.BlockSpec(memory_space=pltpu.SMEM), any_spec, any_spec, any_spec],
        out_specs=any_spec,
        scratch_shapes=[
            pltpu.VMEM((ROWS, PEERS * HD), jnp.bfloat16), pltpu.VMEM((2, ROWS, PEERS * HD), jnp.bfloat16),
            pltpu.VMEM((2, LEN, HD), jnp.bfloat16), pltpu.VMEM((2, SPANS, LEN, HD), jnp.bfloat16),
            pltpu.VMEM((2, LEN, 2 * HD), jnp.bfloat16), pltpu.VMEM((2, LEN, HD), jnp.float32),
            pltpu.VMEM((2, LEN, 2 * HD), jnp.float32), pltpu.VMEM((2, LEN, HD), jnp.bfloat16),
            dma((3,)), dma((2,)), dma((8,)), dma, dma((5,)), dma((8,)), dma((8,)), dma((8,)), dma((32,)), dma, dma],
        compiler_params=pltpu.CompilerParams(collective_id=0, has_side_effects=True, vmem_limit_bytes=VMEM_LIMIT),
        name="span_attention",
    )(token_counts, query_rows, key_rows, value_rows)


def solution(mesh):
    rows = P(("span", "seq"), None)
    return jax.shard_map(
        on_device, mesh=mesh, in_specs=(rows, rows, rows, P()), out_specs=rows, check_vma=False)
```

time: 392 us -> 78.9 us (0.20)
  the two profiles are of different devices: /device:TPU:153 before, /device:TPU:56 now
where the time goes in v1:
time: 78.9 us; the launch traced here: 78.8 us
  Pallas kernels  77 us (98%)
  local copies, waits for them, and re-layouts  1.77 us (2%)
    pallas_call x1, Pallas kernels, on_device(): pl.pallas_call(kernel, out_shape=jax.ShapeDtypeStruct((ROWS, PEERS * HD),...  77 us
    unnamed x1, local copies, waits for them, and re-layouts  1.77 us

profile of v1, /device:TPU:56, one launch (start us, length us, event | category | flops | bytes accessed | tf_op | source)
XLA Modules:
  0.0 78.8 jit_solution(16513063435817563649)
XLA Ops:
  0.0 77.0 %span_attention.1 = bf16[48,4096]{1,0:T(8,128)(2,1)} custom-call(s32[16]{0:T(128)} %counts_ref.1, bf16[48,4096]{1,0:T(8,128)(2,1)} %q_ref.1, bf16[48,4096]{1,0:T(8,128)(2,1)} %k_ref.1, bf16[48,4096]{1,0:T(8,128)(2,1)} %v_ref.1), custom_call_target="tpu_custom_call" | custom-call | tf_op jit(solution)/shard_map/span_attention/pallas_call | solution.py:338
  77.0 1.8 %copy.6 = bf16[48,4096]{1,0:T(8,128)(2,1)} copy(bf16[48,4096]{1,0:T(8,128)(2,1)} %span_attention.1) | data formatting | bytes 786432

commit v2 on v1

--- a/solution.py
+++ b/solution.py
@@ -86,17 +86,14 @@
 HALF = LEN // 2
 
 
-def attend_item(q_index, pair, half, keep_second, counts_ref, q2_ref, kv_ref, m_ref, acc_ref):
+def attend_item(q_index, spans, limits, half, q2_ref, kv_ref, m_ref, acc_ref):
     rows = pl.ds(pl.multiple_of(half * HALF, 16), HALF)
-    first, second = 2 * pair, 2 * pair + 1
-    k = jnp.concatenate([kv_ref[0, first, rows], kv_ref[0, second, rows]], axis=0)
+    k = jnp.concatenate([kv_ref[0, span, rows] for span in spans], axis=0)
     k2 = jnp.concatenate([k, k], axis=1)
-    v = jnp.concatenate([kv_ref[1, first, rows], kv_ref[1, second, rows]], axis=0)
+    v = jnp.concatenate([kv_ref[1, span, rows] for span in spans], axis=0)
     v2 = jnp.concatenate([v, jnp.ones_like(v)], axis=1)
     lane = lax.broadcasted_iota(jnp.int32, (1, HALF), 1) + half * HALF
-    bias = jnp.concatenate([
-        jnp.where(lane < counts_ref[first], 0.0, NEG),
-        jnp.where(lane < counts_ref[second] * keep_second, 0.0, NEG)], axis=1)
+    bias = jnp.concatenate([jnp.where(lane < limit, 0.0, NEG) for limit in limits], axis=1)
     tiles = LEN // TILE
     scores, probs = [None] * tiles, [None] * tiles
 
@@ -129,13 +126,13 @@
             gain(i - 2)
 
 
-def prepare(z_hi, q_ref, q2_ref, m_ref, acc_ref):
-    q = q_ref[z_hi].astype(jnp.float32) * LOG2_SCALE
+def prepare(i, q_ref, q2_ref, m_ref, acc_ref):
+    q = q_ref[i].astype(jnp.float32) * LOG2_SCALE
     high = q.astype(jnp.bfloat16)
     low = (q - high.astype(jnp.float32)).astype(jnp.bfloat16)
-    q2_ref[z_hi] = jnp.concatenate([high, low], axis=1)
-    m_ref[z_hi] = jnp.full((LEN, HD), NEG, jnp.float32)
-    acc_ref[z_hi] = jnp.zeros((LEN, 2 * HD), jnp.float32)
+    q2_ref[i] = jnp.concatenate([high, low], axis=1)
+    m_ref[i] = jnp.full((LEN, HD), NEG, jnp.float32)
+    acc_ref[i] = jnp.zeros((LEN, 2 * HD), jnp.float32)
 
 
 MIRROR = (0, 2, 1, 4, 3, 6, 5, 7)
@@ -146,11 +143,13 @@
 
 
 def kernel(counts_ref, q_ref, k_ref, v_ref, out_ref, stage_q, stage_kv, qall, kvall, q2_ref, m_ref, acc_ref, o_ref,
-           stage_sem, a2a_send, a2a_recv, q_recv, y_send, up_recv, down_recv, far_recv, sib_recv, o_send, o_recv):
+           part_out, part_in, stage_sem, a2a_send, a2a_recv, q_recv, y_send, up_recv, down_recv, far_recv, sib_send,
+           sib_recv, part_recv, o_send, o_recv):
     me = Place()
     up, down, sibling = me.up(), me.down(), me.sibling()
     peers = me.peers()
     own_head = peers[0, 0][1]
+    z_half = me.z // 4
     staged = [
         pltpu.make_async_copy(k_ref, stage_kv.at[0], stage_sem.at[0]),
         pltpu.make_async_copy(v_ref, stage_kv.at[1], stage_sem.at[1]),
@@ -165,8 +164,8 @@
         return pl.ds(pl.multiple_of(head * HD, HD), HD)
 
     rows = pl.ds(pl.multiple_of(me.seq * ROWS, 16), ROWS)
-    kv_rows = kvall.at[:, me.span, rows]
-    q_rows = qall.at[me.z // 4, rows]
+    kv_rows = kvall.at[:, me.span // 2, rows]
+    q_rows = qall.at[2 + z_half, rows]
 
     def send_kv(places):
         for t, dx in places:
@@ -180,63 +179,62 @@
 
     y_up, y_down, y_far = (me.y + 1) % 4, (me.y + 3) % 4, (me.y + 2) % 4
 
-    def block(t, y, core):
+    def block(t, y):
         z = me.plane(t)
         part = pl.ds(pl.multiple_of((z % 4) * PART, 16), PART)
-        return me.span_of(z // 4, y, core), part
+        return (z // 4) * 4 + y, part
 
     def own_part(t):
-        span, part = block(t, me.y, me.core)
+        span, part = block(t, me.y)
         ref = kvall.at[:, span, part]
         arrived(ref, a2a_recv.at[t])
         remote(ref, ref, y_send.at[0], up_recv.at[t], up).start()
         remote(ref, ref, y_send.at[1], down_recv.at[t], down).start()
-        remote(ref, ref, y_send.at[4], sib_recv.at[t], sibling).start()
 
     def near_part(t):
-        span, part = block(t, y_down, me.core)
-        ref = kvall.at[:, span, part]
-        arrived(ref, up_recv.at[t])
+        span, part = block(t, y_down)
+        arrived(kvall.at[:, span, part], up_recv.at[t])
         half = kvall.at[0, span, part]
         remote(half, half, y_send.at[2], far_recv.at[t], up).start()
-        remote(ref, ref, y_send.at[4], sib_recv.at[8 + t], sibling).start()
-        span, part = block(t, y_up, me.core)
-        ref = kvall.at[:, span, part]
-        arrived(ref, down_recv.at[t])
+        span, part = block(t, y_up)
+        arrived(kvall.at[:, span, part], down_recv.at[t])
         half = kvall.at[1, span, part]
         remote(half, half, y_send.at[3], far_recv.at[t], down).start()
-        remote(ref, ref, y_send.at[4], sib_recv.at[16 + t], sibling).start()
 
     def far_part(t):
-        span, part = block(t, y_far, me.core)
-        ref = kvall.at[:, span, part]
-        arrived(ref, far_recv.at[t])
-        remote(ref, ref, y_send.at[4], sib_recv.at[24 + t], sibling).start()
-
-    def from_sibling(j, y, t):
-        span, part = block(t, y, 1 - me.core)
-        arrived(kvall.at[:, span, part], sib_recv.at[8 * j + t])
+        span, part = block(t, y_far)
+        arrived(kvall.at[:, span, part], far_recv.at[t])
 
     def each(first, last, part):
         lax.fori_loop(first, last, lambda t, _: (part(t), 0)[1], 0)
 
     to = cols(own_head)
 
+    def give(h):
+        lane = lax.broadcasted_iota(jnp.int32, (LEN, HD), 1)
+        part_out[h, 0] = acc_ref[h, :, :HD]
+        part_out[h, 1] = jnp.where(lane < HD // 2, m_ref[h], acc_ref[h, :, HD:])
+        remote(part_out.at[h], part_in.at[h], sib_send.at[1 + h], part_recv.at[h], sibling).start()
+
     def finish(h):
-        o_ref[h] = (acc_ref[h, :, :HD] / acc_ref[h, :, HD:]).astype(jnp.bfloat16)
-
-        @pl.when(me.z // 4 == h)
-        def _():
-            piece = o_ref.at[h, rows]
-            pltpu.make_async_copy(piece, out_ref.at[:, to], o_recv).start()
-
-        for place in order:
-            device, head = peers[place]
-
-            @pl.when(head // 16 == h)
-            def _():
-                piece = o_ref.at[h, pl.ds(pl.multiple_of((head % 16) * ROWS, 16), ROWS)]
-                remote(piece, out_ref.at[:, to], o_send, o_recv, device).start()
+        arrived(part_in.at[h], part_recv.at[h])
+        mine, theirs = m_ref[2 + h], part_in[h, 1, :, :1]
+        top = jnp.maximum(mine, theirs)
+        keep, add = jnp.exp2(mine - top), jnp.exp2(theirs - top)
+        total = acc_ref[2 + h, :, HD:] * keep + part_in[h, 1, :, HD // 2:HD // 2 + 1] * add
+        o_ref[h] = ((acc_ref[2 + h, :, :HD] * keep + part_in[h, 0] * add) / total).astype(jnp.bfloat16)
+
+        @pl.when(z_half == h)
+        def _():
+            pltpu.make_async_copy(o_ref.at[h, rows], out_ref.at[:, to], o_recv).start()
+
+        for t in range(8):
+            @pl.when(peers[t, 0][1] // 16 == h)
+            def _():
+                for dx in range(1 if t == 0 else 0, 4):
+                    device, head = peers[t, dx]
+                    piece = o_ref.at[h, pl.ds(pl.multiple_of((head % 16) * ROWS, 16), ROWS)]
+                    remote(piece, out_ref.at[:, to], o_send, o_recv, device).start()
 
     for copy in staged[:2]:
         copy.wait()
@@ -256,66 +254,70 @@
     send_kv(messages(7))
     near_part(1)
     near_part(2)
+    arrived(qall.at[2:4], q_recv)
+    to_sibling = remote(qall.at[2:4], qall.at[0:2], sib_send.at[0], sib_recv, sibling)
+    to_sibling.start()
+    each(2, 4, lambda i: prepare(i, qall, q2_ref, m_ref, acc_ref))
     each(0, 3, far_part)
-    arrived(qall, q_recv)
-    each(0, 2, lambda h: prepare(h, qall, q2_ref, m_ref, acc_ref))
-    each(0, 1, functools.partial(from_sibling, 0, me.y))
-    each(0, 1, functools.partial(from_sibling, 1, y_down))
-    each(0, 1, functools.partial(from_sibling, 2, y_up))
-    each(0, 1, functools.partial(from_sibling, 3, y_far))
+    to_sibling.wait_recv()
+    each(0, 2, lambda i: prepare(i, qall, q2_ref, m_ref, acc_ref))
 
     def step(i, _):
-        g, j = i // 4, i % 4
+        g, second = i // 2, i % 2
         near, far = 2 * g + 1, jnp.minimum(2 * g + 3, 8)
         more, most = 2 * g + 3, jnp.where(g < 3, jnp.minimum(2 * g + 5, 8), 2 * g + 3)
 
-        @pl.when(j == 0)
-        def _():
-            each(near, far, functools.partial(from_sibling, 0, me.y))
-
-        @pl.when(j == 1)
-        def _():
-            each(more, jnp.minimum(more + 1, most), own_part)
-            each(near, far, functools.partial(from_sibling, 1, y_down))
-
-        @pl.when(j == 2)
-        def _():
+        @pl.when((g >= 1) & (second == 0))
+        def _():
+            each(near, far, near_part)
+
+        @pl.when(second == 1)
+        def _():
+            @pl.when(g >= 1)
+            def _():
+                each(near, far, far_part)
+
             each(more + 1, most, own_part)
 
-            @pl.when(g >= 1)
-            def _():
-                each(near, far, far_part)
-
-            each(near, far, functools.partial(from_sibling, 2, y_up))
-
-        @pl.when(j == 3)
-        def _():
-            each(more, most, near_part)
-            each(near, far, functools.partial(from_sibling, 3, y_far))
-
-        y = (me.y + jnp.where(j == 0, 0, jnp.where(j == 1, 3, jnp.where(j == 2, 1, 2)))) % 4
+        @pl.when((i == 7) & (me.z < 4))
+        def _():
+            finish(0)
+
         z_hi, half = me.group(g)
-        pair = z_hi * 4 + y
+        ys = (jnp.where(second == 0, y_down, me.y), jnp.where(second == 0, y_up, y_far))
 
         def item(q_index, _):
-            own = q_index * 4 + me.y
-
-            @pl.when(pair <= own)
-            def _():
-                keep = jnp.where((pair < own) | (me.core == 1), 1, 0)
-                attend_item(q_index, pair, half, keep, counts_ref, q2_ref, kvall, m_ref, acc_ref)
+            @pl.when((second == 0) & (q_index == 2))
+            def _():
+                each(more, jnp.minimum(more + 1, most), own_part)
+
+            h = q_index % 2
+            core = jnp.where(q_index < 2, 1 - me.core, me.core)
+            own = 2 * (h * 4 + me.y) + core
+            spans = [z_hi * 4 + y for y in ys]
+            seen = [2 * span + me.core <= own for span in spans]
+            limits = [jnp.where(see, counts_ref[2 * span + me.core], 0) for see, span in zip(seen, spans)]
+
+            @pl.when(seen[0] | seen[1])
+            def _():
+                attend_item(q_index, spans, limits, half, q2_ref, kvall, m_ref, acc_ref)
+
+            @pl.when((q_index == 0) & (i == jnp.where(me.z < 4, 5, 7)))
+            def _():
+                give(0)
 
             return 0
 
         lax.fori_loop(0, 2, item, 0)
 
-        @pl.when((i == 11) & (me.z < 4))
-        def _():
-            finish(0)
-
+        @pl.when(i == 7)
+        def _():
+            give(1)
+
+        lax.fori_loop(2, 4, item, 0)
         return 0
 
-    lax.fori_loop(0, 16, step, 0)
+    lax.fori_loop(0, 8, step, 0)
 
     @pl.when(me.z >= 4)
     def _():
@@ -326,8 +328,11 @@
     sent = pl.ds(0, (PEERS - 1) * HD)
     arrived(stage_kv.at[:, :, sent], a2a_send.at[0])
     arrived(stage_q.at[:, sent], a2a_send.at[1])
-    for j, ref in enumerate((kvall.at[:, 0:2], kvall.at[:, 0:2], kvall.at[0, 0:2], kvall.at[0, 0:2], kvall.at[:, 0:8])):
+    for j, ref in enumerate((kvall.at[:, 0:2], kvall.at[:, 0:2], kvall.at[0, 0:2], kvall.at[0, 0:2])):
         arrived(ref, y_send.at[j])
+    to_sibling.wait_send()
+    for h in range(2):
+        arrived(part_out.at[h], sib_send.at[1 + h])
     arrived(out_ref, o_recv)
     arrived(out_ref.at[:, sent], o_send)
 
@@ -342,10 +347,12 @@
         out_specs=any_spec,
         scratch_shapes=[
             pltpu.VMEM((ROWS, PEERS * HD), jnp.bfloat16), pltpu.VMEM((2, ROWS, PEERS * HD), jnp.bfloat16),
-            pltpu.VMEM((2, LEN, HD), jnp.bfloat16), pltpu.VMEM((2, SPANS, LEN, HD), jnp.bfloat16),
-            pltpu.VMEM((2, LEN, 2 * HD), jnp.bfloat16), pltpu.VMEM((2, LEN, HD), jnp.float32),
-            pltpu.VMEM((2, LEN, 2 * HD), jnp.float32), pltpu.VMEM((2, LEN, HD), jnp.bfloat16),
-            dma((3,)), dma((2,)), dma((8,)), dma, dma((5,)), dma((8,)), dma((8,)), dma((8,)), dma((32,)), dma, dma],
+            pltpu.VMEM((4, LEN, HD), jnp.bfloat16), pltpu.VMEM((2, SPANS // 2, LEN, HD), jnp.bfloat16),
+            pltpu.VMEM((4, LEN, 2 * HD), jnp.bfloat16), pltpu.VMEM((4, LEN, HD), jnp.float32),
+            pltpu.VMEM((4, LEN, 2 * HD), jnp.float32), pltpu.VMEM((2, LEN, HD), jnp.bfloat16),
+            pltpu.VMEM((2, 2, LEN, HD), jnp.float32), pltpu.VMEM((2, 2, LEN, HD), jnp.float32),
+            dma((3,)), dma((2,)), dma((8,)), dma, dma((4,)), dma((8,)), dma((8,)), dma((8,)), dma((3,)), dma,
+            dma((2,)), dma, dma],
         compiler_params=pltpu.CompilerParams(collective_id=0, has_side_effects=True, vmem_limit_bytes=VMEM_LIMIT),
         name="span_attention",
     )(token_counts, query_rows, key_rows, value_rows)

time: 78.9 us -> 79.4 us (level)
  no operation moved by 1% of the time
where the time goes in v2:
time: 79.4 us; the launch traced here: 78.7 us
  Pallas kernels  77 us (97%)
  local copies, waits for them, and re-layouts  1.77 us (2%)
    pallas_call x1, Pallas kernels, on_device(): pl.pallas_call(kernel, out_shape=jax.ShapeDtypeStruct((ROWS, PEERS * HD),...  77 us
    unnamed x1, local copies, waits for them, and re-layouts  1.77 us

profile of v2, /device:TPU:56, one launch (start us, length us, event | category | flops | bytes accessed | tf_op | source)
XLA Modules:
  0.0 78.7 jit_solution(3180203893727825300)
XLA Ops:
  0.0 77.0 %span_attention.1 = bf16[48,4096]{1,0:T(8,128)(2,1)} custom-call(s32[16]{0:T(128)} %counts_ref.1, bf16[48,4096]{1,0:T(8,128)(2,1)} %q_ref.1, bf16[48,4096]{1,0:T(8,128)(2,1)} %k_ref.1, bf16[48,4096]{1,0:T(8,128)(2,1)} %v_ref.1), custom_call_target="tpu_custom_call" | custom-call | tf_op jit(solution)/shard_map/span_attention/pallas_call | solution.py:343
  77.0 1.8 %copy.6 = bf16[48,4096]{1,0:T(8,128)(2,1)} copy(bf16[48,4096]{1,0:T(8,128)(2,1)} %span_attention.1) | data formatting | bytes 786432

commit v3 on v2

v3 whole, which is shorter than its diff:
```python
import functools
import math

import jax
import jax.numpy as jnp
from jax import lax
from jax.experimental import pallas as pl
from jax.experimental.pallas import tpu as pltpu
from jax.sharding import PartitionSpec as P

MESH = pl.DeviceIdType.MESH
HD = 128
SPANS = 16
LEN = 768
ROWS = 48
PART = 192
PEERS = 32
NEG = -1e30
LOG2_SCALE = HD ** -0.5 * math.log2(math.e)
VMEM_LIMIT = 56 * 1024 * 1024


class Place:
    def __init__(self):
        self.span = lax.axis_index("span")
        self.seq = lax.axis_index("seq")
        self.core = self.span % 2
        self.y = (self.span // 2) % 4
        self.z = (self.span // 8) * 4 + self.seq // 4
        self.x = self.seq % 4

    def span_of(self, z_hi, y, core):
        return (z_hi * 4 + y) * 2 + core

    def plane(self, t):
        return (self.z + ((t + 1) // 2) * (2 * (t % 2) - 1) + 8) % 8

    def turn_of(self, z):
        d = (z - self.z + 8) % 8
        return jnp.where(d > 4, 2 * (8 - d), jnp.maximum(2 * d - 1, 0))

    def peers(self):
        places = {}
        xs = [self.x] + [(self.x + dx) % 4 for dx in (1, 2, 3)]
        for t in range(8):
            dz = ((t + 1) // 2) * (2 * (t % 2) - 1)
            z = (self.z + dz + 8) % 8
            z_hi, z_lo = z // 4, z % 4
            span = self.span_of(z_hi, self.y, self.core)
            for dx in range(4):
                seq = z_lo * 4 + xs[dx]
                places[t, dx] = ((span, seq), z_hi * 16 + seq)
        return places

    def group(self, g):
        z_hi, z_lo = self.z // 4, self.z % 4
        inner = ((z_lo + 1) // 2) % 2
        other = jnp.where(g == 0, 0, jnp.where(g == 1, 1 - inner, jnp.where(g == 2, inner, 1)))
        moved = jnp.where((g == 1) | (g == 2), 1, 0)
        return (z_hi + other) % 2, (z_lo // 2 + moved) % 2

    def up(self):
        return (self.span_of(self.z // 4, (self.y + 1) % 4, self.core), self.seq)

    def down(self):
        return (self.span_of(self.z // 4, (self.y + 3) % 4, self.core), self.seq)

    def sibling(self):
        return (self.span_of(self.z // 4, self.y, 1 - self.core), self.seq)


def greet(devices):
    barrier = pltpu.get_barrier_semaphore()
    for device in devices:
        pl.semaphore_signal(barrier, inc=1, device_id=device, device_id_type=MESH)
    pl.semaphore_wait(barrier, len(devices))


def remote(src, dst, send_sem, recv_sem, device):
    return pltpu.make_async_remote_copy(
        src_ref=src, dst_ref=dst, send_sem=send_sem, recv_sem=recv_sem,
        device_id=device, device_id_type=MESH)


def arrived(ref, sem):
    pltpu.make_async_copy(ref, ref, sem).wait()


TILE = 256
HALF = LEN // 2


def attend_item(q_indices, segments, x, masked, q2_ref, kv_ref, m_ref, acc_ref):
    k = jnp.concatenate([kv_ref[j, t, :, 0].reshape(PART, HD) for j, t, _ in segments], axis=0)
    k2 = jnp.concatenate([k, k], axis=1)
    v = jnp.concatenate([kv_ref[j, t, :, 1].reshape(PART, HD) for j, t, _ in segments], axis=0)
    v2 = jnp.concatenate([v, jnp.ones_like(v)], axis=1)
    if masked:
        lane = lax.broadcasted_iota(jnp.int32, (1, PART), 1)
        turn = sum(jnp.where(lane >= n * ROWS, 1, 0) for n in (1, 2, 3))
        at_x = x + turn
        row = lane + (jnp.where(at_x >= 4, at_x - 4, at_x) - turn) * ROWS
        bias = jnp.concatenate([jnp.where(row < limit, 0.0, NEG) for _, _, limit in segments], axis=1)
    tiles = [(q, pl.ds(i * TILE, TILE)) for q in q_indices for i in range(LEN // TILE)]
    scores, probs, shrinks = {}, {}, {}

    def score(i):
        q, at = tiles[i]
        scores[i] = lax.dot_general(q2_ref[q, at], k2, (((1,), (1,)), ((), ())), preferred_element_type=jnp.float32)

    def soften(i):
        q, at = tiles[i]
        s = scores.pop(i)
        if masked:
            s = s + bias
        m_old = m_ref[q, at]
        m_new = jnp.maximum(m_old, jnp.max(s, axis=1, keepdims=True))
        probs[i] = jnp.exp2(s - jnp.concatenate([m_new] * (LEN // HD), axis=1)).astype(jnp.bfloat16)
        m_ref[q, at] = m_new
        shrinks[i] = jnp.exp2(m_old - m_new)

    def gain(i):
        q, at = tiles[i]
        shrink = shrinks.pop(i)
        acc_ref[q, at] = acc_ref[q, at] * jnp.concatenate([shrink, shrink], axis=1) + jnp.dot(
            probs.pop(i), v2, preferred_element_type=jnp.float32)

    for i in range(len(tiles) + 2):
        if i < len(tiles):
            score(i)
        if 1 <= i < len(tiles) + 1:
            soften(i - 1)
        if 2 <= i:
            gain(i - 2)


def prepare(i, q, q2_ref, m_ref, acc_ref):
    q = q.astype(jnp.float32) * LOG2_SCALE
    high = q.astype(jnp.bfloat16)
    low = (q - high.astype(jnp.float32)).astype(jnp.bfloat16)
    q2_ref[i] = jnp.concatenate([high, low], axis=1)
    m_ref[i] = jnp.full((LEN, HD), NEG, jnp.float32)
    acc_ref[i] = jnp.zeros((LEN, 2 * HD), jnp.float32)


MIRROR = (0, 2, 1, 4, 3, 6, 5, 7)


LEVELS = ((0, 1), (1, 3), (3, 5), (5, 7), (7, 8))


def kernel(counts_ref, q_ref, k_ref, v_ref, out_ref, stage, z_kv, z_q, kv, qall, q2_ref, m_ref, acc_ref, o_ref,
           part_out, part_in, stage_sem, z_send, z_recv, zq_recv, x_send, x_recv, q_recv, y_send, up_recv, down_recv,
           far_recv, sib_send, part_recv, o_send, o_recv):
    me = Place()
    up, down, sibling = me.up(), me.down(), me.sibling()
    peers = me.peers()
    own_head = peers[0, 0][1]
    z_half = me.z // 4
    staged = [pltpu.make_async_copy(ref, stage.at[i], stage_sem.at[i]) for i, ref in enumerate((k_ref, v_ref, q_ref))]
    for copy in staged:
        copy.start()
    across = [(me.span + 1 - 2 * me.core, peers[0, dx][0][1]) for dx in range(4)]
    greet([device for device, _ in list(peers.values())[1:]] + [up, down] + across)

    def cols(head, heads=1):
        return pl.ds(pl.multiple_of(head * HD, HD), heads * HD)

    x_cols = [cols(peers[0, dx][1] - 4 * me.z) for dx in range(4)]

    def send_z_kv(level):
        for t in range(*LEVELS[level]):
            device, head = peers[t, 0]
            there = MIRROR[t]
            remote(stage.at[pl.ds(0, 2), :, cols(head - me.x, 4)], z_kv.at[there], z_send.at[0],
                   z_recv.at[(there + 1) // 2], device).start()

    def send_z_q(level):
        for t in range(*LEVELS[level]):
            device, head = peers[t, 0]
            there = MIRROR[t]
            remote(stage.at[2, :, cols(head - me.x, 4)], z_q.at[there], z_send.at[1],
                   zq_recv.at[0 if there < 5 else 1], device).start()

    def send_x_kv(level):
        t = pl.ds(LEVELS[level][0], LEVELS[level][1] - LEVELS[level][0])
        if level:
            arrived(z_kv.at[t], z_recv.at[level])
        for dx in range(4):
            if level:
                source, place = z_kv.at[t, :, :, x_cols[dx]], kv.at[0, t, (4 - dx) % 4]
            else:
                source, place = stage.at[pl.ds(0, 2), :, cols(peers[0, dx][1])], kv.at[0, 0, (4 - dx) % 4]
            if dx:
                remote(source, place, x_send.at[0], x_recv.at[level], peers[0, dx][0]).start()
            else:
                pltpu.make_async_copy(source, place, x_recv.at[level]).start()

    def send_x_q(part):
        t = (0, pl.ds(1, 4), pl.ds(5, 3))[part]
        if part:
            arrived(z_q.at[t], zq_recv.at[part - 1])
        for dx in range(4):
            source = z_q.at[t, :, x_cols[dx]] if part else stage.at[2, :, cols(peers[0, dx][1])]
            place = qall.at[1, t, (4 - dx) % 4]
            if dx:
                remote(source, place, x_send.at[1], q_recv, peers[0, dx][0]).start()
            else:
                pltpu.make_async_copy(source, place, q_recv).start()
            remote(source, qall.at[0, t, (4 - dx) % 4], x_send.at[2], q_recv, across[dx]).start()

    def own_part(level):
        t = pl.ds(LEVELS[level][0], LEVELS[level][1] - LEVELS[level][0])
        arrived(kv.at[0, t], x_recv.at[level])
        remote(kv.at[0, t], kv.at[1, t], y_send.at[0], up_recv.at[level], up).start()
        remote(kv.at[0, t], kv.at[2, t], y_send.at[1], down_recv.at[level], down).start()

    def near_part(level):
        t = pl.ds(LEVELS[level][0], LEVELS[level][1] - LEVELS[level][0])
        arrived(kv.at[1, t], up_recv.at[level])
        remote(kv.at[1, t, pl.ds(0, 2)], kv.at[3, t, pl.ds(0, 2)], y_send.at[2], far_recv.at[level], up).start()
        arrived(kv.at[2, t], down_recv.at[level])
        remote(kv.at[2, t, pl.ds(2, 2)], kv.at[3, t, pl.ds(2, 2)], y_send.at[3], far_recv.at[level], down).start()

    def far_part(level):
        t = pl.ds(LEVELS[level][0], LEVELS[level][1] - LEVELS[level][0])
        arrived(kv.at[3, t], far_recv.at[level])

    def give(h):
        lane = lax.broadcasted_iota(jnp.int32, (LEN, HD), 1)
        part_out[h, 0] = acc_ref[h, :, :HD]
        part_out[h, 1] = jnp.where(lane < HD // 2, m_ref[h], acc_ref[h, :, HD:])
        remote(part_out.at[h], part_in.at[h], sib_send.at[h], part_recv.at[h], sibling).start()

    to = cols(own_head)

    def finish(h):
        arrived(part_in.at[h], part_recv.at[h])
        mine, theirs = m_ref[2 + h], part_in[h, 1, :, :1]
        top = jnp.maximum(mine, theirs)
        keep, add = jnp.exp2(mine - top), jnp.exp2(theirs - top)
        total = acc_ref[2 + h, :, HD:] * keep + part_in[h, 1, :, HD // 2:HD // 2 + 1] * add
        o_ref[h] = ((acc_ref[2 + h, :, :HD] * keep + part_in[h, 0] * add) / total).astype(jnp.bfloat16)

        for t in range(8):
            @pl.when(peers[t, 0][1] // 16 == h)
            def _():
                first = pl.multiple_of((peers[t, 0][1] % 16) // 4 * PART, 16)
                for s in range(4):
                    piece = o_ref.at[h, pl.ds(first + s * ROWS, ROWS)]
                    if t or s:
                        remote(piece, out_ref.at[:, to], o_send, o_recv, peers[t, s][0]).start()
                    else:
                        pltpu.make_async_copy(piece, out_ref.at[:, to], o_recv).start()

    def prepare_span(k, h):
        q = [qall[k, me.turn_of(4 * h + z_lo)].reshape(PART, HD) for z_lo in range(4)]
        prepare(2 * k + h, jnp.concatenate(q, axis=0), q2_ref, m_ref, acc_ref)

    for copy in staged[:2]:
        copy.wait()
    send_z_kv(1)
    send_x_kv(0)
    staged[2].wait()
    for level in (1, 2, 3, 4):
        send_z_q(level)
    for level in (2, 3, 4):
        send_z_kv(level)
    send_x_q(0)
    own_part(0)
    send_x_kv(1)
    near_part(0)
    own_part(1)
    send_x_q(1)
    near_part(1)
    send_x_q(2)
    far_part(0)
    send_x_kv(2)
    far_part(1)
    arrived(qall, q_recv)
    lax.fori_loop(0, 4, lambda i, _: (prepare_span(i // 2, i % 2), 0)[1], 0)

    before = {1: [(send_x_kv, 3)], 2: [(near_part, 2)], 3: [(far_part, 2), (send_x_kv, 4)], 4: [(near_part, 3)],
              5: [(far_part, 3)], 6: [(near_part, 4)], 7: [(far_part, 4)]}
    amid = {0: [(own_part, 2)], 2: [(own_part, 3)], 4: [(own_part, 4)]}

    def step(i, _):
        g, second = i // 2, i % 2
        for at, events in before.items():
            @pl.when(i == at)
            def _():
                for part, level in events:
                    part(level)

        @pl.when((i == 7) & (me.z < 4))
        def _():
            finish(0)

        z_hi, half = me.group(g)
        plane = z_hi * 4 + half * 2
        turns = (me.turn_of(plane), me.turn_of(plane + 1))
        places = (jnp.where(second == 0, 1, 0), jnp.where(second == 0, 2, 3))
        ys = [(me.y + jnp.where(second == 0, n, f)) % 4 for n, f in ((3, 0), (1, 2))]

        spans = [2 * (z_hi * 4 + y) + me.core for y in ys]
        last = i == 7

        def segments_for(own):
            limits = [jnp.where(span <= own, counts_ref[span], 0) for span in spans]
            return [(j, t, limit - (half * 2 + n) * PART) for j, limit in zip(places, limits) for n, t in enumerate(turns)]

        def both(h, _):
            for at, events in amid.items():
                @pl.when((i == at) & (h == 1))
                def _():
                    for part, level in events:
                        part(level)

            low = 2 * (h * 4 + me.y)
            seen = [span <= low for span in spans]
            alike = [seen[n] | (spans[n] > low + 1) for n in range(2)]
            together = (seen[0] | seen[1]) & alike[0] & alike[1] & jnp.logical_not(last)
            plain = (half == 0) & seen[0] & seen[1]

            @pl.when(together & plain)
            def _():
                attend_item((h, 2 + h), segments_for(low), me.x, False, q2_ref, kv, m_ref, acc_ref)

            @pl.when(together & jnp.logical_not(plain))
            def _():
                attend_item((h, 2 + h), segments_for(low), me.x, True, q2_ref, kv, m_ref, acc_ref)

            @pl.when(jnp.logical_not(together))
            def _():
                lax.fori_loop(0, jnp.where(last, 1, 2), functools.partial(one, h), 0)

            @pl.when((h == 0) & (i == jnp.where(me.z < 4, 5, 7)))
            def _():
                give(0)

            return 0

        def one(h, k, _):
            own = 2 * (h * 4 + me.y) + jnp.where(k == 0, 1 - me.core, me.core)

            @pl.when((spans[0] <= own) | (spans[1] <= own))
            def _():
                attend_item((2 * k + h,), segments_for(own), me.x, True, q2_ref, kv, m_ref, acc_ref)

            return 0

        lax.fori_loop(0, 2, both, 0)

        @pl.when(last)
        def _():
            give(1)
            lax.fori_loop(0, 2, lambda h, _: one(h, 1, 0), 0)

        return 0

    lax.fori_loop(0, 8, step, 0)

    @pl.when(me.z >= 4)
    def _():
        finish(0)

    finish(1)

    arrived(z_kv.at[pl.ds(0, 7)], z_send.at[0])
    arrived(z_q.at[pl.ds(0, 7)], z_send.at[1])
    arrived(kv.at[0, :, pl.ds(0, 3)], x_send.at[0])
    arrived(qall.at[0, :, pl.ds(0, 3)], x_send.at[1])
    for j, ref in enumerate((kv.at[0], kv.at[0], kv.at[0, :, pl.ds(0, 2)], kv.at[0, :, pl.ds(0, 2)])):
        arrived(ref, y_send.at[j])
    arrived(qall.at[0], x_send.at[2])
    for h in range(2):
        arrived(part_out.at[h], sib_send.at[h])
    arrived(out_ref, o_recv)
    arrived(out_ref.at[:, pl.ds(0, (PEERS - 1) * HD)], o_send)


def on_device(query_rows, key_rows, value_rows, token_counts):
    any_spec = pl.BlockSpec(memory_space=pl.ANY)
    dma = pltpu.SemaphoreType.DMA
    return pl.pallas_call(
        kernel,
        out_shape=jax.ShapeDtypeStruct((ROWS, PEERS * HD), jnp.bfloat16),
        in_specs=[pl.BlockSpec(memory_space=pltpu.SMEM), any_spec, any_spec, any_spec],
        out_specs=any_spec,
        scratch_shapes=[
            pltpu.VMEM((3, ROWS, PEERS * HD), jnp.bfloat16), pltpu.VMEM((8, 2, ROWS, 4 * HD), jnp.bfloat16),
            pltpu.VMEM((8, ROWS, 4 * HD), jnp.bfloat16), pltpu.VMEM((4, 8, 4, 2, ROWS, HD), jnp.bfloat16),
            pltpu.VMEM((2, 8, 4, ROWS, HD), jnp.bfloat16),
            pltpu.VMEM((4, LEN, 2 * HD), jnp.bfloat16), pltpu.VMEM((4, LEN, HD), jnp.float32),
            pltpu.VMEM((4, LEN, 2 * HD), jnp.float32), pltpu.VMEM((2, LEN, HD), jnp.bfloat16),
            pltpu.VMEM((2, 2, LEN, HD), jnp.float32), pltpu.VMEM((2, 2, LEN, HD), jnp.float32),
            dma((3,)), dma((2,)), dma((5,)), dma((2,)), dma((3,)), dma((5,)), dma, dma((4,)), dma((5,)), dma((5,)),
            dma((5,)), dma((2,)), dma((2,)), dma, dma],
        compiler_params=pltpu.CompilerParams(collective_id=0, has_side_effects=True, vmem_limit_bytes=VMEM_LIMIT),
        name="span_attention",
    )(token_counts, query_rows, key_rows, value_rows)


def solution(mesh):
    rows = P(("span", "seq"), None)
    return jax.shard_map(
        on_device, mesh=mesh, in_specs=(rows, rows, rows, P()), out_specs=rows, check_vma=False)
```

time: 79.4 us -> 79.5 us (level)
  no operation moved by 1% of the time
where the time goes in v3:
time: 79.5 us; the launch traced here: 78.2 us
  Pallas kernels  76.4 us (96%)
  local copies, waits for them, and re-layouts  1.77 us (2%)
    pallas_call x1, Pallas kernels, on_device(): pl.pallas_call(kernel, out_shape=jax.ShapeDtypeStruct((ROWS, PEERS * HD),...  76.4 us
    unnamed x1, local copies, waits for them, and re-layouts  1.77 us

profile of v3, /device:TPU:56, one launch (start us, length us, event | category | flops | bytes accessed | tf_op | source)
XLA Modules:
  0.0 78.2 jit_solution(166377407148281412)
XLA Ops:
  0.0 76.4 %span_attention.1 = bf16[48,4096]{1,0:T(8,128)(2,1)} custom-call(s32[16]{0:T(128)} %counts_ref.1, bf16[48,4096]{1,0:T(8,128)(2,1)} %q_ref.1, bf16[48,4096]{1,0:T(8,128)(2,1)} %k_ref.1, bf16[48,4096]{1,0:T(8,128)(2,1)} %v_ref.1), custom_call_target="tpu_custom_call" | custom-call | tf_op jit(solution)/shard_map/span_attention/pallas_call | solution.py:385
  76.4 1.8 %copy.6 = bf16[48,4096]{1,0:T(8,128)(2,1)} copy(bf16[48,4096]{1,0:T(8,128)(2,1)} %span_attention.1) | data formatting | bytes 786432

commit v4 on v3

--- a/solution.py
+++ b/solution.py
@@ -28,23 +28,24 @@
         self.y = (self.span // 2) % 4
         self.z = (self.span // 8) * 4 + self.seq // 4
         self.x = self.seq % 4
+        self.sign = 1 - 2 * self.core
 
     def span_of(self, z_hi, y, core):
         return (z_hi * 4 + y) * 2 + core
 
     def plane(self, t):
-        return (self.z + ((t + 1) // 2) * (2 * (t % 2) - 1) + 8) % 8
-
-    def turn_of(self, z):
-        d = (z - self.z + 8) % 8
+        return (self.z + self.sign * ((t + 1) // 2) * (2 * (t % 2) - 1) + 8) % 8
+
+    def turn_of(self, z, sign):
+        d = (sign * (z - self.z) + 8) % 8
         return jnp.where(d > 4, 2 * (8 - d), jnp.maximum(2 * d - 1, 0))
 
     def peers(self):
         places = {}
-        xs = [self.x] + [(self.x + dx) % 4 for dx in (1, 2, 3)]
+        xs = [self.x] + [(self.x + self.sign * dx + 4) % 4 for dx in (1, 2, 3)]
         for t in range(8):
             dz = ((t + 1) // 2) * (2 * (t % 2) - 1)
-            z = (self.z + dz + 8) % 8
+            z = (self.z + self.sign * dz + 8) % 8
             z_hi, z_lo = z // 4, z % 4
             span = self.span_of(z_hi, self.y, self.core)
             for dx in range(4):
@@ -60,10 +61,10 @@
         return (z_hi + other) % 2, (z_lo // 2 + moved) % 2
 
     def up(self):
-        return (self.span_of(self.z // 4, (self.y + 1) % 4, self.core), self.seq)
+        return (self.span_of(self.z // 4, (self.y + self.sign + 4) % 4, self.core), self.seq)
 
     def down(self):
-        return (self.span_of(self.z // 4, (self.y + 3) % 4, self.core), self.seq)
+        return (self.span_of(self.z // 4, (self.y - self.sign + 4) % 4, self.core), self.seq)
 
     def sibling(self):
         return (self.span_of(self.z // 4, self.y, 1 - self.core), self.seq)
@@ -90,7 +91,7 @@
 HALF = LEN // 2
 
 
-def attend_item(q_indices, segments, x, masked, q2_ref, kv_ref, m_ref, acc_ref):
+def attend_item(q_indices, segments, x, sign, masked, q2_ref, kv_ref, m_ref, acc_ref):
     k = jnp.concatenate([kv_ref[j, t, :, 0].reshape(PART, HD) for j, t, _ in segments], axis=0)
     k2 = jnp.concatenate([k, k], axis=1)
     v = jnp.concatenate([kv_ref[j, t, :, 1].reshape(PART, HD) for j, t, _ in segments], axis=0)
@@ -98,8 +99,9 @@
     if masked:
         lane = lax.broadcasted_iota(jnp.int32, (1, PART), 1)
         turn = sum(jnp.where(lane >= n * ROWS, 1, 0) for n in (1, 2, 3))
-        at_x = x + turn
-        row = lane + (jnp.where(at_x >= 4, at_x - 4, at_x) - turn) * ROWS
+        at_x = x + sign * turn
+        at_x = jnp.where(at_x >= 4, at_x - 4, jnp.where(at_x < 0, at_x + 4, at_x))
+        row = lane + (at_x - turn) * ROWS
         bias = jnp.concatenate([jnp.where(row < limit, 0.0, NEG) for _, _, limit in segments], axis=1)
     tiles = [(q, pl.ds(i * TILE, TILE)) for q in q_indices for i in range(LEN // TILE)]
     scores, probs, shrinks = {}, {}, {}
@@ -254,7 +256,7 @@
                         pltpu.make_async_copy(piece, out_ref.at[:, to], o_recv).start()
 
     def prepare_span(k, h):
-        q = [qall[k, me.turn_of(4 * h + z_lo)].reshape(PART, HD) for z_lo in range(4)]
+        q = [qall[k, me.turn_of(4 * h + z_lo, me.sign * (2 * k - 1))].reshape(PART, HD) for z_lo in range(4)]
         prepare(2 * k + h, jnp.concatenate(q, axis=0), q2_ref, m_ref, acc_ref)
 
     for copy in staged[:2]:
@@ -298,9 +300,9 @@
 
         z_hi, half = me.group(g)
         plane = z_hi * 4 + half * 2
-        turns = (me.turn_of(plane), me.turn_of(plane + 1))
+        turns = (me.turn_of(plane, me.sign), me.turn_of(plane + 1, me.sign))
         places = (jnp.where(second == 0, 1, 0), jnp.where(second == 0, 2, 3))
-        ys = [(me.y + jnp.where(second == 0, n, f)) % 4 for n, f in ((3, 0), (1, 2))]
+        ys = [(me.y + jnp.where(second == 0, n * me.sign, f) + 4) % 4 for n, f in ((-1, 0), (1, 2))]
 
         spans = [2 * (z_hi * 4 + y) + me.core for y in ys]
         last = i == 7
@@ -324,11 +326,11 @@
 
             @pl.when(together & plain)
             def _():
-                attend_item((h, 2 + h), segments_for(low), me.x, False, q2_ref, kv, m_ref, acc_ref)
+                attend_item((h, 2 + h), segments_for(low), me.x, me.sign, False, q2_ref, kv, m_ref, acc_ref)
 
             @pl.when(together & jnp.logical_not(plain))
             def _():
-                attend_item((h, 2 + h), segments_for(low), me.x, True, q2_ref, kv, m_ref, acc_ref)
+                attend_item((h, 2 + h), segments_for(low), me.x, me.sign, True, q2_ref, kv, m_ref, acc_ref)
 
             @pl.when(jnp.logical_not(together))
             def _():
@@ -345,7 +347,7 @@
 
             @pl.when((spans[0] <= own) | (spans[1] <= own))
             def _():
-                attend_item((2 * k + h,), segments_for(own), me.x, True, q2_ref, kv, m_ref, acc_ref)
+                attend_item((2 * k + h,), segments_for(own), me.x, me.sign, True, q2_ref, kv, m_ref, acc_ref)
 
             return 0
 

time: 79.5 us -> 79.4 us (level)
  no operation moved by 1% of the time
where the time goes in v4:
time: 79.4 us; the launch traced here: 78.1 us
  Pallas kernels  76.3 us (96%)
  local copies, waits for them, and re-layouts  1.77 us (2%)
    pallas_call x1, Pallas kernels, on_device(): pl.pallas_call(kernel, out_shape=jax.ShapeDtypeStruct((ROWS, PEERS * HD),...  76.3 us
    unnamed x1, local copies, waits for them, and re-layouts  1.77 us

profile of v4, /device:TPU:56, one launch (start us, length us, event | category | flops | bytes accessed | tf_op | source)
XLA Modules:
  0.0 78.1 jit_solution(11353849295548402354)
XLA Ops:
  0.0 76.3 %span_attention.1 = bf16[48,4096]{1,0:T(8,128)(2,1)} custom-call(s32[16]{0:T(128)} %counts_ref.1, bf16[48,4096]{1,0:T(8,128)(2,1)} %q_ref.1, bf16[48,4096]{1,0:T(8,128)(2,1)} %k_ref.1, bf16[48,4096]{1,0:T(8,128)(2,1)} %v_ref.1), custom_call_target="tpu_custom_call" | custom-call | tf_op jit(solution)/shard_map/span_attention/pallas_call | solution.py:387
  76.4 1.8 %copy.6 = bf16[48,4096]{1,0:T(8,128)(2,1)} copy(bf16[48,4096]{1,0:T(8,128)(2,1)} %span_attention.1) | data formatting | bytes 786432

commit v5 on v4

--- a/solution.py
+++ b/solution.py
@@ -87,7 +87,7 @@
     pltpu.make_async_copy(ref, ref, sem).wait()
 
 
-TILE = 256
+TILE = 384
 HALF = LEN // 2
 
 

time: 79.4 us -> 79.4 us (level)
  no operation moved by 1% of the time
where the time goes in v5:
time: 79.4 us; the launch traced here: 78 us
  Pallas kernels  76.2 us (96%)
  local copies, waits for them, and re-layouts  1.77 us (2%)
    pallas_call x1, Pallas kernels, on_device(): pl.pallas_call(kernel, out_shape=jax.ShapeDtypeStruct((ROWS, PEERS * HD),...  76.2 us
    unnamed x1, local copies, waits for them, and re-layouts  1.77 us

profile of v5, /device:TPU:56, one launch (start us, length us, event | category | flops | bytes accessed | tf_op | source)
XLA Modules:
  0.0 78.0 jit_solution(3358757855501566870)
XLA Ops:
  0.0 76.2 %span_attention.1 = bf16[48,4096]{1,0:T(8,128)(2,1)} custom-call(s32[16]{0:T(128)} %counts_ref.1, bf16[48,4096]{1,0:T(8,128)(2,1)} %q_ref.1, bf16[48,4096]{1,0:T(8,128)(2,1)} %k_ref.1, bf16[48,4096]{1,0:T(8,128)(2,1)} %v_ref.1), custom_call_target="tpu_custom_call" | custom-call | tf_op jit(solution)/shard_map/span_attention/pallas_call | solution.py:387
  76.2 1.8 %copy.6 = bf16[48,4096]{1,0:T(8,128)(2,1)} copy(bf16[48,4096]{1,0:T(8,128)(2,1)} %span_attention.1) | data formatting | bytes 786432

commit v6 on v1

--- a/solution.py
+++ b/solution.py
@@ -230,7 +230,7 @@
             piece = o_ref.at[h, rows]
             pltpu.make_async_copy(piece, out_ref.at[:, to], o_recv).start()
 
-        for place in order:
+        for place in reversed(order):
             device, head = peers[place]
 
             @pl.when(head // 16 == h)
@@ -245,9 +245,9 @@
     send_kv(messages(1, 2))
     staged[2].wait()
     pltpu.make_async_copy(stage_q.at[:, to], q_rows, q_recv).start()
-    send_q(order[:15])
+    send_q(order[:14:-1])
     own_part(0)
-    send_q(order[15:])
+    send_q(order[14::-1])
     own_part(1)
     own_part(2)
     send_kv(messages(3, 4))

time: 78.9 us -> 77 us (0.976); the launches traced: 78.8 us -> 75.7 us
  Pallas kernels: 77 us -> 74 us
    pallas_call x1, Pallas kernels: 77 us -> 74 us  [on_device(): pl.pallas_call(kernel, out_shape=jax.ShapeDtypeStruct((ROWS, PEERS * HD),...]
where the time goes in v6:
time: 77 us; the launch traced here: 75.7 us
  Pallas kernels  74 us (96%)
  local copies, waits for them, and re-layouts  1.77 us (2%)
    pallas_call x1, Pallas kernels, on_device(): pl.pallas_call(kernel, out_shape=jax.ShapeDtypeStruct((ROWS, PEERS * HD),...  74 us
    unnamed x1, local copies, waits for them, and re-layouts  1.77 us

profile of v6, /device:TPU:56, one launch (start us, length us, event | category | flops | bytes accessed | tf_op | source)
XLA Modules:
  0.0 75.7 jit_solution(3276721119507776630)
XLA Ops:
  0.0 74.0 %span_attention.1 = bf16[48,4096]{1,0:T(8,128)(2,1)} custom-call(s32[16]{0:T(128)} %counts_ref.1, bf16[48,4096]{1,0:T(8,128)(2,1)} %q_ref.1, bf16[48,4096]{1,0:T(8,128)(2,1)} %k_ref.1, bf16[48,4096]{1,0:T(8,128)(2,1)} %v_ref.1), custom_call_target="tpu_custom_call" | custom-call | tf_op jit(solution)/shard_map/span_attention/pallas_call | solution.py:338
  74.0 1.8 %copy.6 = bf16[48,4096]{1,0:T(8,128)(2,1)} copy(bf16[48,4096]{1,0:T(8,128)(2,1)} %span_attention.1) | data formatting | bytes 786432

commit v7 on v6

--- a/solution.py
+++ b/solution.py
@@ -224,19 +224,21 @@
 
     def finish(h):
         o_ref[h] = (acc_ref[h, :, :HD] / acc_ref[h, :, HD:]).astype(jnp.bfloat16)
-
-        @pl.when(me.z // 4 == h)
-        def _():
-            piece = o_ref.at[h, rows]
-            pltpu.make_async_copy(piece, out_ref.at[:, to], o_recv).start()
-
-        for place in reversed(order):
-            device, head = peers[place]
-
-            @pl.when(head // 16 == h)
-            def _():
-                piece = o_ref.at[h, pl.ds(pl.multiple_of((head % 16) * ROWS, 16), ROWS)]
-                remote(piece, out_ref.at[:, to], o_send, o_recv, device).start()
+        for z_lo in range(4):
+            for dx in range(4):
+                seq = z_lo * 4 + (me.x + dx) % 4
+                device = (me.span_of(h, me.y, me.core), seq)
+                piece = o_ref.at[h, pl.ds(pl.multiple_of(seq * ROWS, 16), ROWS)]
+                own = (me.z == 4 * h + z_lo) if dx == 0 else False
+
+                def send():
+                    remote(piece, out_ref.at[:, to], o_send, o_recv, device).start()
+
+                if dx:
+                    send()
+                else:
+                    pl.when(own)(lambda: pltpu.make_async_copy(piece, out_ref.at[:, to], o_recv).start())
+                    pl.when(jnp.logical_not(own))(send)
 
     for copy in staged[:2]:
         copy.wait()
@@ -265,20 +267,21 @@
     each(0, 1, functools.partial(from_sibling, 3, y_far))
 
     def step(i, _):
-        g, j = i // 4, i % 4
+        again = i >= 16
+        g, j = jnp.minimum(i // 4, 3), i % 4
         near, far = 2 * g + 1, jnp.minimum(2 * g + 3, 8)
         more, most = 2 * g + 3, jnp.where(g < 3, jnp.minimum(2 * g + 5, 8), 2 * g + 3)
 
-        @pl.when(j == 0)
+        @pl.when((j == 0) & jnp.logical_not(again))
         def _():
             each(near, far, functools.partial(from_sibling, 0, me.y))
 
-        @pl.when(j == 1)
+        @pl.when((j == 1) & jnp.logical_not(again))
         def _():
             each(more, jnp.minimum(more + 1, most), own_part)
             each(near, far, functools.partial(from_sibling, 1, y_down))
 
-        @pl.when(j == 2)
+        @pl.when((j == 2) & jnp.logical_not(again))
         def _():
             each(more + 1, most, own_part)
 
@@ -288,7 +291,7 @@
 
             each(near, far, functools.partial(from_sibling, 2, y_up))
 
-        @pl.when(j == 3)
+        @pl.when((j == 3) & jnp.logical_not(again))
         def _():
             each(more, most, near_part)
             each(near, far, functools.partial(from_sibling, 3, y_far))
@@ -307,20 +310,18 @@
 
             return 0
 
-        lax.fori_loop(0, 2, item, 0)
-
-        @pl.when((i == 11) & (me.z < 4))
+        late = me.z >= 4
+        first = jnp.where(again, 1, 0)
+        last = jnp.where(again, jnp.where(late, 2, 1), jnp.where((g == 3) & late, 1, 2))
+        lax.fori_loop(first, last, item, 0)
+
+        @pl.when(i == jnp.where(late, 15, 11))
         def _():
             finish(0)
 
         return 0
 
-    lax.fori_loop(0, 16, step, 0)
-
-    @pl.when(me.z >= 4)
-    def _():
-        finish(0)
-
+    lax.fori_loop(0, 20, step, 0)
     finish(1)
 
     sent = pl.ds(0, (PEERS - 1) * HD)

time: 77 us -> 73.3 us (0.952)
  Pallas kernels: 74 us -> 70.1 us
    pallas_call x1, Pallas kernels: 74 us -> 70.1 us  [on_device(): pl.pallas_call(kernel, out_shape=jax.ShapeDtypeStruct((ROWS, PEERS * HD),...]
where the time goes in v7:
time: 73.3 us; the launch traced here: 71.8 us
  Pallas kernels  70.1 us (96%)
  local copies, waits for them, and re-layouts  1.77 us (2%)
    pallas_call x1, Pallas kernels, on_device(): pl.pallas_call(kernel, out_shape=jax.ShapeDtypeStruct((ROWS, PEERS * HD),...  70.1 us
    unnamed x1, local copies, waits for them, and re-layouts  1.77 us

profile of v7, /device:TPU:56, one launch (start us, length us, event | category | flops | bytes accessed | tf_op | source)
XLA Modules:
  0.0 71.8 jit_solution(16515244602703413151)
XLA Ops:
  0.0 70.1 %span_attention.1 = bf16[48,4096]{1,0:T(8,128)(2,1)} custom-call(s32[16]{0:T(128)} %counts_ref.1, bf16[48,4096]{1,0:T(8,128)(2,1)} %q_ref.1, bf16[48,4096]{1,0:T(8,128)(2,1)} %k_ref.1, bf16[48,4096]{1,0:T(8,128)(2,1)} %v_ref.1), custom_call_target="tpu_custom_call" | custom-call | tf_op jit(solution)/shard_map/span_attention/pallas_call | solution.py:339
  70.1 1.8 %copy.6 = bf16[48,4096]{1,0:T(8,128)(2,1)} copy(bf16[48,4096]{1,0:T(8,128)(2,1)} %span_attention.1) | data formatting | bytes 786432

commit v8 on v7

--- a/solution.py
+++ b/solution.py
@@ -259,6 +259,7 @@
     near_part(1)
     near_part(2)
     each(0, 3, far_part)
+    each(3, 5, own_part)
     arrived(qall, q_recv)
     each(0, 2, lambda h: prepare(h, qall, q2_ref, m_ref, acc_ref))
     each(0, 1, functools.partial(from_sibling, 0, me.y))
@@ -270,30 +271,29 @@
         again = i >= 16
         g, j = jnp.minimum(i // 4, 3), i % 4
         near, far = 2 * g + 1, jnp.minimum(2 * g + 3, 8)
-        more, most = 2 * g + 3, jnp.where(g < 3, jnp.minimum(2 * g + 5, 8), 2 * g + 3)
+        more, most = jnp.minimum(2 * g + 3, 8), jnp.minimum(2 * g + 5, 8)
+        next_more, next_most = jnp.minimum(2 * g + 5, 8), jnp.minimum(2 * g + 7, 8)
 
         @pl.when((j == 0) & jnp.logical_not(again))
         def _():
-            each(near, far, functools.partial(from_sibling, 0, me.y))
-
-        @pl.when((j == 1) & jnp.logical_not(again))
-        def _():
-            each(more, jnp.minimum(more + 1, most), own_part)
-            each(near, far, functools.partial(from_sibling, 1, y_down))
-
-        @pl.when((j == 2) & jnp.logical_not(again))
-        def _():
-            each(more + 1, most, own_part)
-
             @pl.when(g >= 1)
             def _():
                 each(near, far, far_part)
 
+            each(near, far, functools.partial(from_sibling, 0, me.y))
+
+        @pl.when((j == 1) & jnp.logical_not(again))
+        def _():
+            each(more, most, near_part)
+            each(near, far, functools.partial(from_sibling, 1, y_down))
+
+        @pl.when((j == 2) & jnp.logical_not(again))
+        def _():
             each(near, far, functools.partial(from_sibling, 2, y_up))
 
         @pl.when((j == 3) & jnp.logical_not(again))
         def _():
-            each(more, most, near_part)
+            each(next_more, next_most, own_part)
             each(near, far, functools.partial(from_sibling, 3, y_far))
 
         y = (me.y + jnp.where(j == 0, 0, jnp.where(j == 1, 3, jnp.where(j == 2, 1, 2)))) % 4

time: 73.3 us -> 73.5 us (level); the launches traced: 71.8 us -> 73.3 us
  Pallas kernels: 70.1 us -> 71.5 us
    pallas_call x1, Pallas kernels: 70.1 us -> 71.5 us  [on_device(): pl.pallas_call(kernel, out_shape=jax.ShapeDtypeStruct((ROWS, PEERS * HD),...]
where the time goes in v8:
time: 73.5 us; the launch traced here: 73.3 us
  Pallas kernels  71.5 us (97%)
  local copies, waits for them, and re-layouts  1.77 us (2%)
    pallas_call x1, Pallas kernels, on_device(): pl.pallas_call(kernel, out_shape=jax.ShapeDtypeStruct((ROWS, PEERS * HD),...  71.5 us
    unnamed x1, local copies, waits for them, and re-layouts  1.77 us

profile of v8, /device:TPU:56, one launch (start us, length us, event | category | flops | bytes accessed | tf_op | source)
XLA Modules:
  0.0 73.3 jit_solution(7311177847650102355)
XLA Ops:
  0.0 71.5 %span_attention.1 = bf16[48,4096]{1,0:T(8,128)(2,1)} custom-call(s32[16]{0:T(128)} %counts_ref.1, bf16[48,4096]{1,0:T(8,128)(2,1)} %q_ref.1, bf16[48,4096]{1,0:T(8,128)(2,1)} %k_ref.1, bf16[48,4096]{1,0:T(8,128)(2,1)} %v_ref.1), custom_call_target="tpu_custom_call" | custom-call | tf_op jit(solution)/shard_map/span_attention/pallas_call | solution.py:339
  71.5 1.8 %copy.6 = bf16[48,4096]{1,0:T(8,128)(2,1)} copy(bf16[48,4096]{1,0:T(8,128)(2,1)} %span_attention.1) | data formatting | bytes 786432

commit v9 on v8

--- a/solution.py
+++ b/solution.py
@@ -86,19 +86,20 @@
 HALF = LEN // 2
 
 
-def attend_item(q_index, pair, half, keep_second, counts_ref, q2_ref, kv_ref, m_ref, acc_ref):
+def attend_item(q_index, pair, half, keep_second, masked, counts_ref, q2_ref, kv_ref, m_ref, acc_ref):
     rows = pl.ds(pl.multiple_of(half * HALF, 16), HALF)
     first, second = 2 * pair, 2 * pair + 1
     k = jnp.concatenate([kv_ref[0, first, rows], kv_ref[0, second, rows]], axis=0)
     k2 = jnp.concatenate([k, k], axis=1)
     v = jnp.concatenate([kv_ref[1, first, rows], kv_ref[1, second, rows]], axis=0)
     v2 = jnp.concatenate([v, jnp.ones_like(v)], axis=1)
-    lane = lax.broadcasted_iota(jnp.int32, (1, HALF), 1) + half * HALF
-    bias = jnp.concatenate([
-        jnp.where(lane < counts_ref[first], 0.0, NEG),
-        jnp.where(lane < counts_ref[second] * keep_second, 0.0, NEG)], axis=1)
+    if masked:
+        lane = lax.broadcasted_iota(jnp.int32, (1, HALF), 1) + half * HALF
+        bias = jnp.concatenate([
+            jnp.where(lane < counts_ref[first], 0.0, NEG),
+            jnp.where(lane < counts_ref[second] * keep_second, 0.0, NEG)], axis=1)
     tiles = LEN // TILE
-    scores, probs = [None] * tiles, [None] * tiles
+    scores, probs, shrinks = [None] * tiles, [None] * tiles, [None] * tiles
 
     def at(i):
         return pl.ds(i * TILE, TILE)
@@ -108,17 +109,18 @@
             q2_ref[q_index, at(i)], k2, (((1,), (1,)), ((), ())), preferred_element_type=jnp.float32)
 
     def soften(i):
-        s = scores[i] + bias
+        s = scores[i] + bias if masked else scores[i]
         m_old = m_ref[q_index, at(i)]
         m_new = jnp.maximum(m_old, jnp.max(s, axis=1, keepdims=True))
         wide = jnp.concatenate([m_new] * (LEN // HD), axis=1)
         probs[i] = jnp.exp2(s - wide).astype(jnp.bfloat16)
         m_ref[q_index, at(i)] = m_new
-        shrink = jnp.exp2(m_old - m_new)
-        acc_ref[q_index, at(i)] = acc_ref[q_index, at(i)] * jnp.concatenate([shrink, shrink], axis=1)
+        shrinks[i] = jnp.exp2(m_old - m_new)
 
     def gain(i):
-        acc_ref[q_index, at(i)] += jnp.dot(probs[i], v2, preferred_element_type=jnp.float32)
+        shrink = jnp.concatenate([shrinks[i], shrinks[i]], axis=1)
+        acc_ref[q_index, at(i)] = acc_ref[q_index, at(i)] * shrink + jnp.dot(
+            probs[i], v2, preferred_element_type=jnp.float32)
 
     for i in range(tiles + 2):
         if i < tiles:
@@ -303,11 +305,14 @@
         def item(q_index, _):
             own = q_index * 4 + me.y
 
-            @pl.when(pair <= own)
-            def _():
-                keep = jnp.where((pair < own) | (me.core == 1), 1, 0)
-                attend_item(q_index, pair, half, keep, counts_ref, q2_ref, kvall, m_ref, acc_ref)
-
+            keep = (pair < own) | (me.core == 1)
+            plain = keep & (half == 0)
+
+            def work(masked):
+                attend_item(q_index, pair, half, jnp.where(keep, 1, 0), masked, counts_ref, q2_ref, kvall, m_ref, acc_ref)
+
+            pl.when((pair <= own) & plain)(lambda: work(False))
+            pl.when((pair <= own) & jnp.logical_not(plain))(lambda: work(True))
             return 0
 
         late = me.z >= 4

time: 73.5 us -> 73.6 us (level)
  no operation moved by 1% of the time
where the time goes in v9:
time: 73.6 us; the launch traced here: 73.3 us
  Pallas kernels  71.5 us (97%)
  local copies, waits for them, and re-layouts  1.77 us (2%)
    pallas_call x1, Pallas kernels, on_device(): pl.pallas_call(kernel, out_shape=jax.ShapeDtypeStruct((ROWS, PEERS * HD),...  71.5 us
    unnamed x1, local copies, waits for them, and re-layouts  1.77 us

profile of v9, /device:TPU:56, one launch (start us, length us, event | category | flops | bytes accessed | tf_op | source)
XLA Modules:
  0.0 73.3 jit_solution(14096484231206283365)
XLA Ops:
  0.0 71.5 %span_attention.1 = bf16[48,4096]{1,0:T(8,128)(2,1)} custom-call(s32[16]{0:T(128)} %counts_ref.1, bf16[48,4096]{1,0:T(8,128)(2,1)} %q_ref.1, bf16[48,4096]{1,0:T(8,128)(2,1)} %k_ref.1, bf16[48,4096]{1,0:T(8,128)(2,1)} %v_ref.1), custom_call_target="tpu_custom_call" | custom-call | tf_op jit(solution)/shard_map/span_attention/pallas_call | solution.py:344
  71.5 1.8 %copy.6 = bf16[48,4096]{1,0:T(8,128)(2,1)} copy(bf16[48,4096]{1,0:T(8,128)(2,1)} %span_attention.1) | data formatting | bytes 786432

commit v10 on v8

--- a/solution.py
+++ b/solution.py
@@ -247,15 +247,14 @@
     send_kv(messages(1, 2))
     staged[2].wait()
     pltpu.make_async_copy(stage_q.at[:, to], q_rows, q_recv).start()
-    send_q(order[:14:-1])
+    send_q(order[::-1])
+    send_kv(messages(3, 4))
+    send_kv(messages(5, 6))
+    send_kv(messages(7))
     own_part(0)
-    send_q(order[14::-1])
     own_part(1)
     own_part(2)
-    send_kv(messages(3, 4))
     near_part(0)
-    send_kv(messages(5, 6))
-    send_kv(messages(7))
     near_part(1)
     near_part(2)
     each(0, 3, far_part)

time: 73.5 us -> 73.5 us (level)
  no operation moved by 1% of the time
where the time goes in v10:
time: 73.5 us; the launch traced here: 73.3 us
  Pallas kernels  71.5 us (97%)
  local copies, waits for them, and re-layouts  1.77 us (2%)
    pallas_call x1, Pallas kernels, on_device(): pl.pallas_call(kernel, out_shape=jax.ShapeDtypeStruct((ROWS, PEERS * HD),...  71.5 us
    unnamed x1, local copies, waits for them, and re-layouts  1.77 us

profile of v10, /device:TPU:56, one launch (start us, length us, event | category | flops | bytes accessed | tf_op | source)
XLA Modules:
  0.0 73.3 jit_solution(17109479625949878686)
XLA Ops:
  0.0 71.5 %span_attention.1 = bf16[48,4096]{1,0:T(8,128)(2,1)} custom-call(s32[16]{0:T(128)} %counts_ref.1, bf16[48,4096]{1,0:T(8,128)(2,1)} %q_ref.1, bf16[48,4096]{1,0:T(8,128)(2,1)} %k_ref.1, bf16[48,4096]{1,0:T(8,128)(2,1)} %v_ref.1), custom_call_target="tpu_custom_call" | custom-call | tf_op jit(solution)/shard_map/span_attention/pallas_call | solution.py:338
  71.5 1.8 %copy.6 = bf16[48,4096]{1,0:T(8,128)(2,1)} copy(bf16[48,4096]{1,0:T(8,128)(2,1)} %span_attention.1) | data formatting | bytes 786432

commit v11 on v10

--- a/solution.py
+++ b/solution.py
@@ -248,9 +248,9 @@
     staged[2].wait()
     pltpu.make_async_copy(stage_q.at[:, to], q_rows, q_recv).start()
     send_q(order[::-1])
+    send_kv(messages(7))
+    send_kv(messages(5, 6))
     send_kv(messages(3, 4))
-    send_kv(messages(5, 6))
-    send_kv(messages(7))
     own_part(0)
     own_part(1)
     own_part(2)

time: 73.5 us -> 79.9 us (1.087)
  Pallas kernels: 71.5 us -> 77.7 us
    pallas_call x1, Pallas kernels: 71.5 us -> 77.7 us  [on_device(): pl.pallas_call(kernel, out_shape=jax.ShapeDtypeStruct((ROWS, PEERS * HD),...]
where the time goes in v11:
time: 79.9 us; the launch traced here: 79.5 us
  Pallas kernels  77.7 us (97%)
  local copies, waits for them, and re-layouts  1.77 us (2%)
    pallas_call x1, Pallas kernels, on_device(): pl.pallas_call(kernel, out_shape=jax.ShapeDtypeStruct((ROWS, PEERS * HD),...  77.7 us
    unnamed x1, local copies, waits for them, and re-layouts  1.77 us

profile of v11, /device:TPU:56, one launch (start us, length us, event | category | flops | bytes accessed | tf_op | source)
XLA Modules:
  0.0 79.5 jit_solution(3541925380039545914)
XLA Ops:
  0.0 77.7 %span_attention.1 = bf16[48,4096]{1,0:T(8,128)(2,1)} custom-call(s32[16]{0:T(128)} %counts_ref.1, bf16[48,4096]{1,0:T(8,128)(2,1)} %q_ref.1, bf16[48,4096]{1,0:T(8,128)(2,1)} %k_ref.1, bf16[48,4096]{1,0:T(8,128)(2,1)} %v_ref.1), custom_call_target="tpu_custom_call" | custom-call | tf_op jit(solution)/shard_map/span_attention/pallas_call | solution.py:338
  77.7 1.8 %copy.6 = bf16[48,4096]{1,0:T(8,128)(2,1)} copy(bf16[48,4096]{1,0:T(8,128)(2,1)} %span_attention.1) | data formatting | bytes 786432

commit v12 on v10

--- a/solution.py
+++ b/solution.py
@@ -245,10 +245,10 @@
     pltpu.make_async_copy(stage_kv.at[:, :, to], kv_rows, a2a_recv.at[0]).start()
     send_kv(messages(0))
     send_kv(messages(1, 2))
+    send_kv(messages(3, 4))
     staged[2].wait()
     pltpu.make_async_copy(stage_q.at[:, to], q_rows, q_recv).start()
     send_q(order[::-1])
-    send_kv(messages(3, 4))
     send_kv(messages(5, 6))
     send_kv(messages(7))
     own_part(0)

time: 73.5 us -> 71 us (0.966)
  Pallas kernels: 71.5 us -> 68.6 us
    pallas_call x1, Pallas kernels: 71.5 us -> 68.6 us  [on_device(): pl.pallas_call(kernel, out_shape=jax.ShapeDtypeStruct((ROWS, PEERS * HD),...]
where the time goes in v12:
time: 71 us; the launch traced here: 70.4 us
  Pallas kernels  68.6 us (97%)
  local copies, waits for them, and re-layouts  1.77 us (2%)
    pallas_call x1, Pallas kernels, on_device(): pl.pallas_call(kernel, out_shape=jax.ShapeDtypeStruct((ROWS, PEERS * HD),...  68.6 us
    unnamed x1, local copies, waits for them, and re-layouts  1.77 us

profile of v12, /device:TPU:56, one launch (start us, length us, event | category | flops | bytes accessed | tf_op | source)
XLA Modules:
  0.0 70.4 jit_solution(9304097485442738899)
XLA Ops:
  0.0 68.6 %span_attention.1 = bf16[48,4096]{1,0:T(8,128)(2,1)} custom-call(s32[16]{0:T(128)} %counts_ref.1, bf16[48,4096]{1,0:T(8,128)(2,1)} %q_ref.1, bf16[48,4096]{1,0:T(8,128)(2,1)} %k_ref.1, bf16[48,4096]{1,0:T(8,128)(2,1)} %v_ref.1), custom_call_target="tpu_custom_call" | custom-call | tf_op jit(solution)/shard_map/span_attention/pallas_call | solution.py:338
  68.6 1.8 %copy.6 = bf16[48,4096]{1,0:T(8,128)(2,1)} copy(bf16[48,4096]{1,0:T(8,128)(2,1)} %span_attention.1) | data formatting | bytes 786432
